TPU v7x, 32 devices: a whole 2x2x4 slice. The times are simulated.
32 devices in a mesh: dp: 8 (over y, x, core), mp: 4 (over z).
Axes of the slice: x: 2, y: 2, z: 4, core: 2. Of those that a mesh axis runs over, the one named last changes fastest.
Arguments:
- tokens: bfloat16 [32, 1024, 512], P('dp'), may hold values from -6 to 6
- segment_ids: int32 [32, 1024], P('dp'), may hold values from 0 to 3, never falling along the last dimension, each value on 1 to 512 neighbouring positions
- pad_lengths: int32 [32], P('dp'), may hold values from 0 to 255
- cotangent: bfloat16 [32, 1024, 512], P('dp'), may hold values from -6 to 6
- w_qkv: float32 [512, 3, 512], P('dp', None, 'mp'), may hold values from -0.25 to 0.25
- w_out: float32 [512, 512], P('mp', 'dp'), may hold values from -2 to 2
- w_up: float32 [512, 2048], P('dp', 'mp'), may hold values from -0.25 to 0.25
- w_down: float32 [2048, 512], P('mp', 'dp'), may hold values from -0.125 to 0.125
- qv_bias: float32 [2, 8, 64], P(None, 'mp', 'dp'), may hold values from -3 to 3
- ff_bias: float32 [32, 64], P('mp', 'dp'), may hold values from -3 to 3
- norm_gains: float32 [2, 512], P(None, 'dp'), may hold values from 0.5 to 1.5
- norm_shifts: float32 [4, 512], P(None, 'dp'), may hold values from -2 to 2
- first_qkv: float32 [512, 3, 512], P('dp', None, 'mp'), may hold values from -64 to 64
- first_out: float32 [512, 512], P('mp', 'dp'), may hold values from -64 to 64
- first_up: float32 [512, 2048], P('dp', 'mp'), may hold values from -64 to 64
- first_down: float32 [2048, 512], P('mp', 'dp'), may hold values from -64 to 64
- first_qv_bias: float32 [2, 8, 64], P(None, 'mp', 'dp'), may hold values from -64 to 64
- first_ff_bias: float32 [32, 64], P('mp', 'dp'), may hold values from -64 to 64
- first_gains: float32 [2, 512], P(None, 'dp'), may hold values from -64 to 64
- first_shifts: float32 [4, 512], P(None, 'dp'), may hold values from -64 to 64
- second_qkv: float32 [512, 3, 512], P('dp', None, 'mp'), may hold values from 8.192 to 32.768
- second_out: float32 [512, 512], P('mp', 'dp'), may hold values from 8.192 to 32.768
- second_up: float32 [512, 2048], P('dp', 'mp'), may hold values from 8.192 to 32.768
- second_down: float32 [2048, 512], P('mp', 'dp'), may hold values from 8.192 to 32.768
- second_qv_bias: float32 [2, 8, 64], P(None, 'mp', 'dp'), may hold values from 8.192 to 32.768
- second_ff_bias: float32 [32, 64], P('mp', 'dp'), may hold values from 8.192 to 32.768
- second_gains: float32 [2, 512], P(None, 'dp'), may hold values from 8.192 to 32.768
- second_shifts: float32 [4, 512], P(None, 'dp'), may hold values from 8.192 to 32.768
Outputs:
- layer_out: bfloat16 [32, 1024, 512], P('dp')
- tokens_grad: float32 [32, 1024, 512], P('dp')
- next_w_qkv: float32 [512, 3, 512], P('dp', None, 'mp')
- next_w_out: float32 [512, 512], P('mp', 'dp')
- next_w_up: float32 [512, 2048], P('dp', 'mp')
- next_w_down: float32 [2048, 512], P('mp', 'dp')
- next_qv_bias: float32 [2, 8, 64], P(None, 'mp', 'dp')
- next_ff_bias: float32 [32, 64], P('mp', 'dp')
- next_gains: float32 [2, 512], P(None, 'dp')
- next_shifts: float32 [4, 512], P(None, 'dp')
- next_first_qkv: float32 [512, 3, 512], P('dp', None, 'mp')
- next_first_out: float32 [512, 512], P('mp', 'dp')
- next_first_up: float32 [512, 2048], P('dp', 'mp')
- next_first_down: float32 [2048, 512], P('mp', 'dp')
- next_first_qv_bias: float32 [2, 8, 64], P(None, 'mp', 'dp')
- next_first_ff_bias: float32 [32, 64], P('mp', 'dp')
- next_first_gains: float32 [2, 512], P(None, 'dp')
- next_first_shifts: float32 [4, 512], P(None, 'dp')
- next_second_qkv: float32 [512, 3, 512], P('dp', None, 'mp')
- next_second_out: float32 [512, 512], P('mp', 'dp')
- next_second_up: float32 [512, 2048], P('dp', 'mp')
- next_second_down: float32 [2048, 512], P('mp', 'dp')
- next_second_qv_bias: float32 [2, 8, 64], P(None, 'mp', 'dp')
- next_second_ff_bias: float32 [32, 64], P('mp', 'dp')
- next_second_gains: float32 [2, 512], P(None, 'dp')
- next_second_shifts: float32 [4, 512], P(None, 'dp')
Inputs may be any that keep to these rules, and one draw needn't show every extreme that they name: `segment_ids`: within a row the ids never fall; a segment covers at most 512 positions, and one segment of every row exactly that many. The last pad_lengths positions of a row are padding.
All inputs are finite; a program needn't handle non-finite values.
Results may differ from a plain program's by a relative error of at most 0.015.
The roundings to bfloat16 on the way count: a program that leaves them out, or rounds other values in their place, can miss the bound.
Values may be sent and summed in bfloat16 or wider, within the bound.
No kernel may reach another device: no remote copies, remote signals or barrier semaphores. Data moves between devices by JAX's collectives and lax.ppermute only.
A program may use at most 192 MiB of HBM per device.

v0:
```python
import jax
import jax.numpy as jnp
from jax import lax
from jax.sharding import PartitionSpec as P

D = 512
HEADS = 8
HEAD_DIM = 64
FF = 2048
LEN = 1024
MICRO = 2
STEP = 10
QBLOCK = 512


beta_one = 0.9
beta_two = 0.999


def gelu_exact(value):
    return value * 0.5 * (1.0 + lax.erf(value * 0.7071067811865476))


def gelu_slope(value):
    cumulative = 0.5 * (1.0 + lax.erf(value * 0.7071067811865476))
    return cumulative + value * jnp.exp(-0.5 * value * value) * 0.3989422804014327


def norm_forward(value, gain, shift):
    center = value - jnp.mean(value, axis=-1, keepdims=True)
    spread = jnp.mean(center * center, axis=-1, keepdims=True)
    inverse = lax.rsqrt(spread + 1e-05)
    normal = center * inverse
    return (normal * gain + shift, normal, inverse)


def norm_backward(upstream, normal, inverse, gain):
    scaled = upstream * gain
    return inverse * (
        scaled
        - jnp.mean(scaled, axis=-1, keepdims=True)
        - normal * jnp.mean(scaled * normal, axis=-1, keepdims=True)
    )


def masked_scores(queries_low, keys_low, seg_rows, valid_len, offset):
    block_q = lax.dynamic_slice_in_dim(queries_low, offset, QBLOCK, 1)
    raw_scores = (
        jnp.einsum("sqhd,skhd->shqk", block_q, keys_low, preferred_element_type=jnp.float32) * 0.125
    )
    query_seg = lax.dynamic_slice_in_dim(seg_rows, offset, QBLOCK, 1)
    query_pos = offset + jnp.arange(QBLOCK, dtype=jnp.int32)
    key_pos = jnp.arange(seg_rows.shape[1], dtype=jnp.int32)
    same_segment = query_seg[:, :, None] == seg_rows[:, None, :]
    inside = key_pos[None, None, :] < valid_len[:, None, None]
    itself = query_pos[:, None] == key_pos[None, :]
    allowed = same_segment & inside | itself[None]
    return (jnp.where(allowed[:, None], raw_scores, -1e30), block_q)


def adam_step(weight, grad_sum, first, second, rate, decay):
    first_new = beta_one * first + (1.0 - beta_one) * grad_sum
    second_new = beta_two * second + (1.0 - beta_two) * grad_sum * grad_sum
    first_hat = first_new / (1.0 - beta_one**STEP)
    second_hat = second_new / (1.0 - beta_two**STEP)
    weight_new = weight - rate * (first_hat / (jnp.sqrt(second_hat) + 1e-08) + decay * weight)
    return (weight_new, first_new, second_new)


def per_device(
    tokens,
    segment_ids,
    pad_lengths,
    cotangent,
    w_qkv,
    w_out,
    w_up,
    w_down,
    qv_bias,
    ff_bias,
    norm_gains,
    norm_shifts,
    first_qkv,
    first_out,
    first_up,
    first_down,
    first_qv_bias,
    first_ff_bias,
    first_gains,
    first_shifts,
    second_qkv,
    second_out,
    second_up,
    second_down,
    second_qv_bias,
    second_ff_bias,
    second_gains,
    second_shifts,
):
    masters = (w_qkv, w_out, w_up, w_down, qv_bias, ff_bias, norm_gains, norm_shifts)
    copies = [master.astype(jnp.bfloat16) for master in masters]
    gathered = (
        lax.all_gather(copies[0], "dp", axis=0, tiled=True),
        lax.all_gather(copies[1], "dp", axis=1, tiled=True),
        lax.all_gather(copies[2], "dp", axis=0, tiled=True),
        lax.all_gather(copies[3], "dp", axis=1, tiled=True),
        lax.all_gather(copies[4], "dp", axis=2, tiled=True),
        lax.all_gather(copies[5], "dp", axis=1, tiled=True),
        lax.all_gather(copies[6], "dp", axis=1, tiled=True),
        lax.all_gather(copies[7], "dp", axis=1, tiled=True),
    )
    tensor_size = lax.axis_size("mp")
    heads_local = HEADS // tensor_size
    width_local = heads_local * HEAD_DIM
    ff_local = FF // tensor_size
    qkv_full = gathered[0].reshape(D, 3 * width_local)
    out_full = gathered[1]
    up_full = gathered[2]
    down_full = gathered[3]
    bias_pair = gathered[4].astype(jnp.float32)
    ff_shift = gathered[5].astype(jnp.float32).reshape(ff_local)
    gain_rows = gathered[6].astype(jnp.float32)
    shift_rows = gathered[7].astype(jnp.float32)
    offsets = jnp.arange(LEN // QBLOCK, dtype=jnp.int32) * QBLOCK
    rows_micro = tokens.shape[0] // MICRO
    token_count = rows_micro * LEN
    outputs = []
    input_grads = []
    summed = None
    for micro_index in range(MICRO):
        row_begin = micro_index * rows_micro
        token_rows = tokens[row_begin : row_begin + rows_micro]
        seg_rows = segment_ids[row_begin : row_begin + rows_micro]
        valid_len = LEN - pad_lengths[row_begin : row_begin + rows_micro]
        upstream = (
            cotangent[row_begin : row_begin + rows_micro]
            .reshape(token_count, D)
            .astype(jnp.float32)
        )
        flat_rows = token_rows.reshape(token_count, D)
        projected = jnp.dot(flat_rows, qkv_full, preferred_element_type=jnp.float32).reshape(
            rows_micro, LEN, 3, heads_local, HEAD_DIM
        )
        queries_low = (projected[:, :, 0] + bias_pair[0]).astype(jnp.bfloat16)
        keys_low = projected[:, :, 1].astype(jnp.bfloat16)
        values_low = (projected[:, :, 2] + bias_pair[1]).astype(jnp.bfloat16)

        def forward_block(offset):
            scores, block_q = masked_scores(queries_low, keys_low, seg_rows, valid_len, offset)
            row_top = jnp.max(scores, axis=-1, keepdims=True)
            row_sum = jnp.sum(jnp.exp(scores - row_top), axis=-1, keepdims=True)
            log_total = row_top + jnp.log(row_sum)
            probs_low = jnp.exp(scores - log_total).astype(jnp.bfloat16)
            mixed_block = jnp.einsum(
                "shqk,skhd->sqhd", probs_low, values_low, preferred_element_type=jnp.float32
            )
            return (mixed_block, log_total)

        mixed_heads, log_totals = lax.map(forward_block, offsets)
        heads_out = (
            jnp.moveaxis(mixed_heads, 0, 1).reshape(token_count, width_local).astype(jnp.bfloat16)
        )
        attn_part = jnp.dot(heads_out, out_full, preferred_element_type=jnp.float32)
        attention = lax.psum(attn_part, "mp") + shift_rows[0]
        normed, normal_one, inverse_one = norm_forward(
            flat_rows.astype(jnp.float32) + attention, gain_rows[0], shift_rows[2]
        )
        normed_low = normed.astype(jnp.bfloat16)
        pre_act = jnp.dot(normed_low, up_full, preferred_element_type=jnp.float32) + ff_shift
        hidden = gelu_exact(pre_act).astype(jnp.bfloat16)
        ffn_part = jnp.dot(hidden, down_full, preferred_element_type=jnp.float32)
        branch = lax.psum(ffn_part, "mp") + shift_rows[1]
        final, normal_two, inverse_two = norm_forward(normed + branch, gain_rows[1], shift_rows[3])
        g_final = norm_backward(upstream, normal_two, inverse_two, gain_rows[1])
        final_low = final.astype(jnp.bfloat16)
        g_final_low = g_final.astype(jnp.bfloat16)
        outputs.append(final_low.reshape(rows_micro, LEN, D))
        grad_down = jnp.einsum("nf,nd->fd", hidden, g_final_low, preferred_element_type=jnp.float32)
        g_hidden = jnp.einsum(
            "nd,fd->nf", g_final_low, down_full, preferred_element_type=jnp.float32
        )
        g_pre = (g_hidden * gelu_slope(pre_act)).astype(jnp.bfloat16)
        grad_ff = jnp.sum(g_pre.astype(jnp.float32), axis=0)
        grad_up = jnp.einsum("nd,nf->df", normed_low, g_pre, preferred_element_type=jnp.float32)
        normed_part = jnp.einsum("nf,df->nd", g_pre, up_full, preferred_element_type=jnp.float32)
        g_normed = g_final + lax.psum(normed_part, "mp")
        g_attention = norm_backward(g_normed, normal_one, inverse_one, gain_rows[0])
        g_attention_low = g_attention.astype(jnp.bfloat16)
        grad_out = jnp.einsum(
            "nc,nd->cd", heads_out, g_attention_low, preferred_element_type=jnp.float32
        )
        g_heads = (
            jnp.einsum("nd,cd->nc", g_attention_low, out_full, preferred_element_type=jnp.float32)
            .astype(jnp.bfloat16)
            .reshape(rows_micro, LEN, heads_local, HEAD_DIM)
        )

        def backward_block(carry, inputs):
            key_grad, value_grad = carry
            offset, log_total = inputs
            scores, block_q = masked_scores(queries_low, keys_low, seg_rows, valid_len, offset)
            probs_full = jnp.exp(scores - log_total)
            probs_low = probs_full.astype(jnp.bfloat16)
            block_grad = lax.dynamic_slice_in_dim(g_heads, offset, QBLOCK, 1)
            value_grad = value_grad + jnp.einsum(
                "shqk,sqhd->skhd", probs_low, block_grad, preferred_element_type=jnp.float32
            )
            g_probs = jnp.einsum(
                "sqhd,skhd->shqk", block_grad, values_low, preferred_element_type=jnp.float32
            )
            row_delta = jnp.sum(g_probs * probs_full, axis=-1, keepdims=True)
            g_raw = (probs_full * (g_probs - row_delta) * 0.125).astype(jnp.bfloat16)
            query_block = jnp.einsum(
                "shqk,skhd->sqhd", g_raw, keys_low, preferred_element_type=jnp.float32
            )
            key_grad = key_grad + jnp.einsum(
                "shqk,sqhd->skhd", g_raw, block_q, preferred_element_type=jnp.float32
            )
            return ((key_grad, value_grad), query_block)

        empty_grad = jnp.zeros((rows_micro, LEN, heads_local, HEAD_DIM), jnp.float32)
        (key_grad, value_grad), query_blocks = lax.scan(
            backward_block, (empty_grad, empty_grad), (offsets, log_totals)
        )
        query_grad = jnp.moveaxis(query_blocks, 0, 1).reshape(
            rows_micro, LEN, heads_local, HEAD_DIM
        )
        grads_low = jnp.stack([query_grad, key_grad, value_grad], axis=2).astype(jnp.bfloat16)
        grad_bias = jnp.sum(grads_low[:, :, 0::2].astype(jnp.float32), axis=(0, 1))
        flat_grads = grads_low.reshape(token_count, 3 * width_local)
        grad_qkv = jnp.einsum(
            "nd,nc->dc", flat_rows, flat_grads, preferred_element_type=jnp.float32
        ).reshape(D, 3, width_local)
        token_part = jnp.einsum(
            "nc,dc->nd", flat_grads, qkv_full, preferred_element_type=jnp.float32
        )
        grad_gains = jnp.stack(
            [jnp.sum(g_normed * normal_one, axis=0), jnp.sum(upstream * normal_two, axis=0)]
        )
        grad_shifts = jnp.stack(
            [
                jnp.sum(g_attention, axis=0),
                jnp.sum(g_final, axis=0),
                jnp.sum(g_normed, axis=0),
                jnp.sum(upstream, axis=0),
            ]
        )
        token_grad = g_attention + lax.psum(token_part.astype(jnp.bfloat16), "mp").astype(
            jnp.float32
        )
        input_grads.append(token_grad.reshape(rows_micro, LEN, D))
        micro_grads = (
            grad_qkv,
            grad_out,
            grad_up,
            grad_down,
            grad_bias,
            grad_ff.reshape(ff_local // HEAD_DIM, HEAD_DIM),
            grad_gains,
            grad_shifts,
        )
        summed = (
            micro_grads
            if summed is None
            else tuple((earlier + fresh_part for earlier, fresh_part in zip(summed, micro_grads)))
        )
    final_grads = (
        lax.psum_scatter(summed[0], "dp", scatter_dimension=0, tiled=True),
        lax.psum_scatter(summed[1], "dp", scatter_dimension=1, tiled=True),
        lax.psum_scatter(summed[2], "dp", scatter_dimension=0, tiled=True),
        lax.psum_scatter(summed[3], "dp", scatter_dimension=1, tiled=True),
        lax.psum_scatter(summed[4], "dp", scatter_dimension=2, tiled=True),
        lax.psum_scatter(summed[5], "dp", scatter_dimension=1, tiled=True),
        lax.psum_scatter(summed[6], "dp", scatter_dimension=1, tiled=True),
        lax.psum_scatter(summed[7], "dp", scatter_dimension=1, tiled=True),
    )
    step_rates = (D ** (-0.5), (D // 64) ** (-0.5), D ** (-0.5), FF ** (-0.5), 0.3, 0.3, 0.3, 0.3)
    decays = (0.01, 0.01, 0.01, 0.01, 0.0, 0.0, 0.0, 0.0)
    firsts = (
        first_qkv,
        first_out,
        first_up,
        first_down,
        first_qv_bias,
        first_ff_bias,
        first_gains,
        first_shifts,
    )
    seconds = (
        second_qkv,
        second_out,
        second_up,
        second_down,
        second_qv_bias,
        second_ff_bias,
        second_gains,
        second_shifts,
    )
    updated = [
        adam_step(
            masters[slot],
            final_grads[slot],
            firsts[slot],
            seconds[slot],
            step_rates[slot],
            decays[slot],
        )
        for slot in range(8)
    ]
    layer_out = jnp.concatenate(outputs, axis=0)
    tokens_grad = jnp.concatenate(input_grads, axis=0)
    new_weights = [entry[0] for entry in updated]
    new_firsts = [entry[1] for entry in updated]
    new_seconds = [entry[2] for entry in updated]
    return tuple([layer_out, tokens_grad] + new_weights + new_firsts + new_seconds)


def solution(mesh):
    return jax.shard_map(
        per_device,
        mesh=mesh,
        in_specs=(
            P("dp", None, None),
            P("dp", None),
            P("dp"),
            P("dp", None, None),
            P("dp", None, "mp"),
            P("mp", "dp"),
            P("dp", "mp"),
            P("mp", "dp"),
            P(None, "mp", "dp"),
            P("mp", "dp"),
            P(None, "dp"),
            P(None, "dp"),
            P("dp", None, "mp"),
            P("mp", "dp"),
            P("dp", "mp"),
            P("mp", "dp"),
            P(None, "mp", "dp"),
            P("mp", "dp"),
            P(None, "dp"),
            P(None, "dp"),
            P("dp", None, "mp"),
            P("mp", "dp"),
            P("dp", "mp"),
            P("mp", "dp"),
            P(None, "mp", "dp"),
            P("mp", "dp"),
            P(None, "dp"),
            P(None, "dp"),
        ),
        out_specs=(
            P("dp", None, None),
            P("dp", None, None),
            P("dp", None, "mp"),
            P("mp", "dp"),
            P("dp", "mp"),
            P("mp", "dp"),
            P(None, "mp", "dp"),
            P("mp", "dp"),
            P(None, "dp"),
            P(None, "dp"),
            P("dp", None, "mp"),
            P("mp", "dp"),
            P("dp", "mp"),
            P("mp", "dp"),
            P(None, "mp", "dp"),
            P("mp", "dp"),
            P(None, "dp"),
            P(None, "dp"),
            P("dp", None, "mp"),
            P("mp", "dp"),
            P("dp", "mp"),
            P("mp", "dp"),
            P(None, "mp", "dp"),
            P("mp", "dp"),
            P(None, "dp"),
            P(None, "dp"),
        ),
        check_vma=False,
    )
```

profile of v0, /device:TPU:0, one launch (start us, length us, event | category | flops | bytes accessed | tf_op | source)
XLA Modules:
  0.0 1653.8 jit_solution(656554336459874869)
XLA Ops:
  8.2 11.0 all_gather.24
  19.4 4.4 fusion.188
  26.8 9.1 all_gather.25
  36.0 8.2 all_gather.26
  50.6 25.8 %while.55 = (s32[]{:T(128)}, bf16[2,2,512,2,64]{2,4,3,1,0:T(8,128)(2,1)}, f32[2,2,2,512,1]{3,2,1,4,0:T(2,128)S(1)}, s32[2]{0:T(128)S(1)}, s32[2,1024]{1,0:T(2,12...) while((s32[]{:T(128)}, ...), condition=%wide.region_13.14_spmd, body=%wide.region_10.13_spmd.sunk | while | flops 563610112 | bytes 36532476 | solution.py:159
  82.3 26.1 %while.54 = (s32[]{:T(128)}, bf16[2,2,512,2,64]{2,4,3,1,0:T(8,128)(2,1)}, f32[2,2,2,512,1]{3,2,1,4,0:T(2,128)S(1)}, s32[2]{0:T(128)S(1)}, s32[2,1024]{1,0:T(2,12...) while((s32[]{:T(128)}, ...), condition=%wide.region_3.4_spmd, body=%wide.region_0.3_spmd.sunk | while | flops 563610112 | bytes 36532476 | solution.py:159
  116.9 8.7 all-gather.1
  125.7 7.9 all-gather
  133.7 8.9 all_gather.30
  142.8 9.9 all_gather.31
  152.7 11.1 all_gather.29
  163.8 4.0 fusion.240
  167.8 240.4 %all-reduce.16.cloned.1.call-done = (f32[2048,512]{1,0:T(8,128)}, f32[2048,512]{1,0:T(8,128)}) async-done(((f32[2048,512]{1,0:T(8,128)}, f32[2048,512]{1,0:T(8,128)}), (f32[2048,512]{1,0:T(8,128)}, f32[2048,512]{1,0:T(8,128)})) %all-reduce.16.cloned.1.call-update) | async-done | bytes 8388624 | tf_op jit(solution)/shard_map/psum | solution.py:164
  408.2 5.2 fusion.238
  419.7 4.2 multiply_convert_fusion.3
  430.9 4.7 convert_reduce_fusion
  435.7 285.8 %all-reduce.14.cloned.1.call-done = (f32[2048,512]{1,0:T(8,128)}, f32[2048,512]{1,0:T(8,128)}) async-done(((f32[2048,512]{1,0:T(8,128)}, f32[2048,512]{1,0:T(8,128)}), (f32[2048,512]{1,0:T(8,128)}, f32[2048,512]{1,0:T(8,128)})) %all-reduce.14.cloned.1.call-update) | async-done | bytes 8388624 | tf_op jit(solution)/shard_map/psum | solution.py:172
  721.4 7.1 fusion.236
  730.7 4.3 fusion.185
  735.0 6.3 fusion.224
  757.9 4.3 fusion.207
  771.4 276.9 %all-reduce.12.cloned.1.call-done = (f32[2048,512]{1,0:T(8,128)}, f32[2048,512]{1,0:T(8,128)}) async-done(((f32[2048,512]{1,0:T(8,128)}, f32[2048,512]{1,0:T(8,128)}), (f32[2048,512]{1,0:T(8,128)}, f32[2048,512]{1,0:T(8,128)})) %all-reduce.12.cloned.1.call-update) | async-done | bytes 8388624 | tf_op jit(solution)/shard_map/psum | solution.py:186
  1048.3 6.7 multiply_reduce_fusion.3
  1058.0 4.7 fusion.226
  1071.1 123.2 %while.56 = (s32[]{:T(128)}, f32[2,1024,2,64]{1,3,2,0:T(8,128)}, f32[2,1024,2,64]{1,3,2,0:T(8,128)}, bf16[2,2,512,2,64]{2,4,3,1,0:T(8,128)(2,1)}, s32[2]{0:T(128...) while((s32[]{:T(128)}, f32[2,1024,2,64]{1,3,2,0:T(8,128)}, ...), condition=%wide.region_27.28_spmd.clone, body=%wide.region_25.27_spmd.clone.sunk | while | flops 1401430528 | bytes 140595472 | solution.py:222
  1081.2 4.8 fusion.358
  1086.0 22.6 %fusion.362 = bf16[2,2,512,2,64]{2,4,3,1,0:T(8,128)(2,1)} fusion(bf16[2,2,512,2,64]{2,4,3,1,0:T(8,128)(2,1)} %get-tuple-element.1076, s32[]{:T(128)S(6)} %copy.209, bf16[2,1024,2,64]{1,3,2,0:T(8,128)(2,1)S(1)} %get-tuple-element.1096, f32[2,2,512,1024]{3,2,1,0:T(8,128)} %fusion.358, f32[2,2,512,1024]{3,2,1,0:T(8,128)} %copy-done, ...), kind=kOutput, calls=%fused_computation.65.clone.1 | convolution fusion | flops 291507200 | bytes 36716548 | tf_op jit(solution)/shard_map/while/body/eval_jaxpr/shqk,skhd->sqhd/dot_general | solution.py:213
  1108.6 23.5 %fusion.360 = f32[2,1024,2,64]{1,3,2,0:T(8,128)} fusion(f32[2,2,512,1024]{3,2,1,0:T(8,128)} %fusion.358, f32[2,2,512,1024]{3,2,1,0:T(8,128)} %copy-done, f32[2,2,512]{2,1,0:T(2,128)S(1)} %dynamic-slice_bitcast_fusion.4, pred[2,512,1024]{2,1,0:T(8,128)(4,1)S(1)} %and_or_fusion.10, f32[2,1024,2,64]{1,3,2,0:T(8,128)} %get-tuple-element.1074, ...), kind=kOutput, calls=%fused_computation.62.clone.1 | convolution fusion | flops 292031488 | bytes 38027268 | tf_op jit(solution)/shard_map/while/body/eval_jaxpr/shqk,sqhd->skhd/dot_general | solution.py:216
  1138.1 5.0 fusion.361
  1143.2 4.8 fusion.358
  1147.9 22.6 %fusion.362 = bf16[2,2,512,2,64]{2,4,3,1,0:T(8,128)(2,1)} fusion(bf16[2,2,512,2,64]{2,4,3,1,0:T(8,128)(2,1)} %get-tuple-element.1076, s32[]{:T(128)S(6)} %copy.209, bf16[2,1024,2,64]{1,3,2,0:T(8,128)(2,1)S(1)} %get-tuple-element.1096, f32[2,2,512,1024]{3,2,1,0:T(8,128)} %fusion.358, f32[2,2,512,1024]{3,2,1,0:T(8,128)} %copy-done, ...), kind=kOutput, calls=%fused_computation.65.clone.1 | convolution fusion | flops 291507200 | bytes 36716548 | tf_op jit(solution)/shard_map/while/body/eval_jaxpr/shqk,skhd->sqhd/dot_general | solution.py:213
  1170.6 23.7 %fusion.360 = f32[2,1024,2,64]{1,3,2,0:T(8,128)} fusion(f32[2,2,512,1024]{3,2,1,0:T(8,128)} %fusion.358, f32[2,2,512,1024]{3,2,1,0:T(8,128)} %copy-done, f32[2,2,512]{2,1,0:T(2,128)S(1)} %dynamic-slice_bitcast_fusion.4, pred[2,512,1024]{2,1,0:T(8,128)(4,1)S(1)} %and_or_fusion.10, f32[2,1024,2,64]{1,3,2,0:T(8,128)} %get-tuple-element.1074, ...), kind=kOutput, calls=%fused_computation.62.clone.1 | convolution fusion | flops 292031488 | bytes 38027268 | tf_op jit(solution)/shard_map/while/body/eval_jaxpr/shqk,sqhd->skhd/dot_general | solution.py:216
  1200.7 123.3 %while.57 = (s32[]{:T(128)}, f32[2,1024,2,64]{1,3,2,0:T(8,128)}, f32[2,1024,2,64]{1,3,2,0:T(8,128)}, bf16[2,2,512,2,64]{2,4,3,1,0:T(8,128)(2,1)}, s32[2]{0:T(128...) while((s32[]{:T(128)}, f32[2,1024,2,64]{1,3,2,0:T(8,128)}, ...), condition=%wide.region_36.37_spmd.clone, body=%wide.region_34.36_spmd.clone.sunk | while | flops 1401430528 | bytes 140595472 | solution.py:222
  1210.6 4.8 fusion.373
  1215.4 22.6 %fusion.377 = bf16[2,2,512,2,64]{2,4,3,1,0:T(8,128)(2,1)} fusion(bf16[2,2,512,2,64]{2,4,3,1,0:T(8,128)(2,1)} %get-tuple-element.1031, s32[]{:T(128)S(6)} %copy.197, bf16[2,1024,2,64]{1,3,2,0:T(8,128)(2,1)S(1)} %get-tuple-element.1051, f32[2,2,512,1024]{3,2,1,0:T(8,128)} %fusion.373, f32[2,2,512,1024]{3,2,1,0:T(8,128)} %copy-done.1, ...), kind=kOutput, calls=%fused_computation.113.clone.1 | convolution fusion | flops 291507200 | bytes 36716548 | tf_op jit(solution)/shard_map/while/body/eval_jaxpr/shqk,skhd->sqhd/dot_general | solution.py:213
  1238.0 23.5 %fusion.375 = f32[2,1024,2,64]{1,3,2,0:T(8,128)} fusion(f32[2,2,512,1024]{3,2,1,0:T(8,128)} %fusion.373, f32[2,2,512,1024]{3,2,1,0:T(8,128)} %copy-done.1, f32[2,2,512]{2,1,0:T(2,128)S(1)} %dynamic-slice_bitcast_fusion.5, pred[2,512,1024]{2,1,0:T(8,128)(4,1)S(1)} %and_or_fusion.11, f32[2,1024,2,64]{1,3,2,0:T(8,128)} %get-tuple-element.1029, ...), kind=kOutput, calls=%fused_computation.110.clone.1 | convolution fusion | flops 292031488 | bytes 38027268 | tf_op jit(solution)/shard_map/while/body/eval_jaxpr/shqk,sqhd->skhd/dot_general | solution.py:216
  1267.6 5.1 fusion.376
  1272.6 4.8 fusion.373
  1277.4 22.6 %fusion.377 = bf16[2,2,512,2,64]{2,4,3,1,0:T(8,128)(2,1)} fusion(bf16[2,2,512,2,64]{2,4,3,1,0:T(8,128)(2,1)} %get-tuple-element.1031, s32[]{:T(128)S(6)} %copy.197, bf16[2,1024,2,64]{1,3,2,0:T(8,128)(2,1)S(1)} %get-tuple-element.1051, f32[2,2,512,1024]{3,2,1,0:T(8,128)} %fusion.373, f32[2,2,512,1024]{3,2,1,0:T(8,128)} %copy-done.1, ...), kind=kOutput, calls=%fused_computation.113.clone.1 | convolution fusion | flops 291507200 | bytes 36716548 | tf_op jit(solution)/shard_map/while/body/eval_jaxpr/shqk,skhd->sqhd/dot_general | solution.py:213
  1300.1 23.7 %fusion.375 = f32[2,1024,2,64]{1,3,2,0:T(8,128)} fusion(f32[2,2,512,1024]{3,2,1,0:T(8,128)} %fusion.373, f32[2,2,512,1024]{3,2,1,0:T(8,128)} %copy-done.1, f32[2,2,512]{2,1,0:T(2,128)S(1)} %dynamic-slice_bitcast_fusion.5, pred[2,512,1024]{2,1,0:T(8,128)(4,1)S(1)} %and_or_fusion.11, f32[2,1024,2,64]{1,3,2,0:T(8,128)} %get-tuple-element.1029, ...), kind=kOutput, calls=%fused_computation.110.clone.1 | convolution fusion | flops 292031488 | bytes 38027268 | tf_op jit(solution)/shard_map/while/body/eval_jaxpr/shqk,sqhd->skhd/dot_general | solution.py:216
  1353.9 4.2 convolution_convert_fusion.1
  1362.1 4.6 pad_maximum_fusion.1
  1370.9 13.9 all-reduce.2
  1389.7 13.4 reduce-scatter.23.cloned.1.call-done
  1405.3 34.5 %reduce-scatter.15.cloned.1.call-done = f32[128,64]{0,1:T(8,128)} async-done(((f32[128,512]{0,1:T(8,128)}), f32[128,64]{0,1:T(8,128)}) %reduce-scatter.15.cloned.1.call-update) | async-done | bytes 32784 | tf_op jit(solution)/shard_map/reduce_scatter | solution.py:269
  1441.3 37.1 %reduce-scatter.13.cloned.1.call-done = f32[64,3,128]{2,0,1:T(8,128)} async-done(((f32[512,3,128]{2,0,1:T(8,128)}), f32[64,3,128]{2,0,1:T(8,128)}) %reduce-scatter.13.cloned.1.call-update) | async-done | bytes 98320 | tf_op jit(solution)/shard_map/reduce_scatter | solution.py:268
  1480.1 156.6 %all-reduce.18.cloned.1.call-done = (bf16[2048,512]{1,0:T(8,128)(2,1)}, bf16[2048,512]{1,0:T(8,128)(2,1)}) async-done(((bf16[2048,512]{1,0:T(8,128)(2,1)}, bf16[2048,512]{1,0:T(8,128)(2,1)}), (bf16[2048,512]{1,0:T(8,128)(2,1)}, bf16[2048,512]{1,0:T(8,128)(2,1)})) %all-reduce.18.cloned.1.call-update) | async-done | bytes 4194320 | tf_op jit(solution)/shard_map/psum | solution.py:248
  1642.1 4.4 pad_maximum_fusion
  (425 shorter events, 203.7 us)
Async XLA Ops:
  7.2 401.0 %all-reduce.16.cloned.1.call-start = ((), (), s32[]{:S(2)}) async-start(), calls=%async_computation.14 | async-start | bytes 16777216 | tf_op jit(solution)/shard_map/psum | solution.py:164
  19.4 7.2 copy-start.62
  76.4 5.9 copy-start.15
  76.4 5.9 copy-start.17
  76.4 5.9 copy-start.30
  76.4 5.9 copy-start.44
  76.4 5.9 copy-start.65
  76.5 5.9 copy-start.69
  108.4 7.7 copy-start.32
  116.1 9.6 copy-start.86
  116.2 26.6 %copy-start.60 = (f32[64,512]{1,0:T(8,128)S(1)}, f32[64,512]{1,0:T(8,128)}, u32[]{:S(2)}) copy-start(f32[64,512]{1,0:T(8,128)} %param.42) | copy-start | bytes 393220
  116.2 26.6 %copy-start.58 = (f32[512,64]{0,1:T(8,128)S(1)}, f32[512,64]{0,1:T(8,128)}, u32[]{:S(2)}) copy-start(f32[512,64]{0,1:T(8,128)} %param.43) | copy-start | bytes 393220
  116.2 605.2 %all-reduce.14.cloned.1.call-start = ((), (), s32[]{:S(2)}) async-start(), calls=%async_computation.13 | async-start | bytes 16777216 | tf_op jit(solution)/shard_map/psum | solution.py:172
  167.8 245.6 %copy-start.26 = (bf16[2,1024,512]{2,1,0:T(8,128)(2,1)}, bf16[2,1024,512]{2,1,0:T(8,128)(2,1)S(1)}, u32[]{:S(2)}) copy-start(bf16[2,1024,512]{2,1,0:T(8,128)(2,1)S(1)} %get-tuple-element.628) | copy-start | bytes 6291460
  430.7 617.6 %all-reduce.12.cloned.1.call-start = ((), (), s32[]{:S(2)}) async-start(), calls=%async_computation.12 | async-start | bytes 16777216 | tf_op jit(solution)/shard_map/psum | solution.py:186
  735.0 6.3 copy-start.29
  735.0 6.3 copy-start.41
  741.3 7.0 copy-start.19
  757.6 609.2 %reduce-scatter.19.cloned.1.call-start = ((), (), s32[]{:S(2)}) async-start(), calls=%async_computation.9 | async-start | bytes 1179648 | tf_op jit(solution)/shard_map/reduce_scatter | solution.py:271
  765.2 603.4 %reduce-scatter.17.cloned.1.call-start = ((), (), s32[]{:S(2)}) async-start(), calls=%async_computation.8 | async-start | bytes 1179648 | tf_op jit(solution)/shard_map/reduce_scatter | solution.py:270
  771.3 616.3 %reduce-scatter.21.cloned.1.call-start = ((), (), s32[]{:S(2)}) async-start(), calls=%async_computation.10 | async-start | bytes 294912
  1048.3 6.8 copy-start.3
  1048.3 7.1 copy-start.5
  1048.3 8.4 copy-start.14
  1048.3 9.7 copy-start.43
  1062.7 5.7 copy-start.8
  1194.3 6.3 copy-start.16
  1194.3 6.3 copy-start.18
  1194.3 6.3 copy-start.31
  1194.3 6.3 copy-start.45
  1194.3 6.3 copy-start.66
  1194.3 6.3 copy-start.70
  1200.6 123.4 %copy-start.82 = (f32[512]{0:T(512)S(1)}, f32[512]{0:T(512)}, u32[]{:S(2)}) copy-start(f32[512]{0:T(512)} %get-tuple-element.464) | copy-start | bytes 6148
  1200.6 123.4 %copy-start.83 = (f32[512]{0:T(512)S(1)}, f32[512]{0:T(512)}, u32[]{:S(2)}) copy-start(f32[512]{0:T(512)} %get-tuple-element.467) | copy-start | bytes 6148
  1200.6 123.4 %copy-start.84 = (f32[512]{0:T(512)S(1)}, f32[512]{0:T(512)}, u32[]{:S(2)}) copy-start(f32[512]{0:T(512)} %get-tuple-element.462) | copy-start | bytes 6148
  1200.6 123.4 %copy-start.85 = (f32[512]{0:T(512)S(1)}, f32[512]{0:T(512)}, u32[]{:S(2)}) copy-start(f32[512]{0:T(512)} %get-tuple-element.652) | copy-start | bytes 6148
  1324.0 6.8 copy-start.39
  1324.9 5.8 copy-start.9
  1333.4 69.7 %reduce-scatter.23.cloned.1.call-start = ((), (), s32[]{:S(2)}) async-start(), calls=%async_computation.11 | async-start | bytes 294912
  1336.2 103.6 %reduce-scatter.15.cloned.1.call-start = ((), (), s32[]{:S(2)}) async-start(), calls=%async_computation.7 | async-start | bytes 294912 | tf_op jit(solution)/shard_map/reduce_scatter | solution.py:269
  1342.5 135.8 %reduce-scatter.13.cloned.1.call-start = ((), (), s32[]{:S(2)}) async-start(), calls=%async_computation.6 | async-start | bytes 884736 | tf_op jit(solution)/shard_map/reduce_scatter | solution.py:268
  1353.5 283.1 %all-reduce.18.cloned.1.call-start = ((), (), s32[]{:S(2)}) async-start(), calls=%async_computation.15 | async-start | bytes 8388608 | tf_op jit(solution)/shard_map/psum | solution.py:248
  1362.1 6.5 copy-start.61
  1362.1 22.7 %copy-start.89 = (f32[2,2,8]{2,1,0:T(2,128)S(1)}, f32[2,2,8]{2,1,0:T(2,128)}, u32[]{:S(2)}) copy-start(f32[2,2,8]{2,1,0:T(2,128)} %param.44) | copy-start | bytes 388
  1362.1 24.1 %copy-start.72 = (f32[8,8]{1,0:T(8,128)S(1)}, f32[8,8]{1,0:T(8,128)}, u32[]{:S(2)}) copy-start(f32[8,8]{1,0:T(8,128)} %param.45) | copy-start | bytes 772
  1362.1 41.9 %copy-start.87 = (f32[4,64]{1,0:T(4,128)S(1)}, f32[4,64]{1,0:T(4,128)}, u32[]{:S(2)}) copy-start(f32[4,64]{1,0:T(4,128)} %param.47) | copy-start | bytes 3076
  1362.1 77.7 %copy-start.68 = (f32[128,64]{0,1:T(8,128)S(1)}, f32[128,64]{0,1:T(8,128)}, u32[]{:S(2)}) copy-start(f32[128,64]{0,1:T(8,128)} %param.41) | copy-start | bytes 98308
  1366.8 111.6 %copy-start.64 = (f32[64,3,128]{2,0,1:T(8,128)S(1)}, f32[64,3,128]{2,0,1:T(8,128)}, u32[]{:S(2)}) copy-start(f32[64,3,128]{2,0,1:T(8,128)} %param.40) | copy-start | bytes 294916
  (64 other events, 205.1 us)
Sparse Core Ops, SparseCore 0:
  116.3 291.8 all-reduce.15
  430.8 290.5 all-reduce.13
  757.7 290.5 all-reduce.11
  1051.3 35.0 reduce-scatter.18
  1089.4 36.2 reduce-scatter.16
  1333.6 32.5 reduce-scatter.20
  1369.5 33.6 reduce-scatter.22
  1406.2 33.6 reduce-scatter.14
  1443.3 34.9 reduce-scatter.12
  1481.3 155.3 all-reduce.17
where the time goes:
time: 1660 us; the launch traced here: 1650 us
  waiting for transfers between devices  1040 us (63%)
  matrix products  315 us (19%)
  other arithmetic  113 us (7%)
  blocking collectives  88.7 us (5%)
  local copies, waits for them, and re-layouts  57.8 us (3%)
  loops' own time  17 us (1%)
    psum x1, waiting for transfers between devices, per_device(): branch = lax.psum(ffn_part, 'mp') + shift_rows[1]  286 us
    psum x1, waiting for transfers between devices, per_device(): g_normed = g_final + lax.psum(normed_part, 'mp')  277 us
    psum x1, waiting for transfers between devices, per_device(): attention = lax.psum(attn_part, 'mp') + shift_rows[0]  240 us
    psum x1, waiting for transfers between devices, per_device(): lax.psum(token_part.astype(jnp.bfloat16), 'mp').astype(jnp.float32)  157 us
    dot_general x4, matrix products, backward_block(): jnp.einsum('shqk,sqhd->skhd', g_raw, block_q, preferred_element_type=jnp....  94.4 us
    dot_general x4, matrix products, backward_block(): jnp.einsum('shqk,skhd->sqhd', g_raw, keys_low, preferred_element_type=jnp...  90.5 us
    reduce_scatter x1, waiting for transfers between devices, per_device(): lax.psum_scatter(summed[0], 'dp', scatter_dimension=0, tiled=True)  37.1 us
    reduce_scatter x1, waiting for transfers between devices, per_device(): lax.psum_scatter(summed[1], 'dp', scatter_dimension=1, tiled=True)  34.5 us
  transfers between devices with their start and end apart: 10, of which 7 were waited for; matrix products, arithmetic and copies ran while one was open for 20% of the time, Pallas kernels for 0%

commit v1 on v0

v1 whole, which is shorter than its diff:
```python
import functools

import jax
import jax.numpy as jnp
from jax import lax
from jax.experimental import pallas as pl
from jax.experimental.pallas import tpu as pltpu
from jax.sharding import PartitionSpec as P

D = 512
HEADS = 8
HEAD_DIM = 64
FF = 2048
LEN = 1024
STEP = 10
PAIR = 128
TILE = 256
FAR = 1e30

beta_one = 0.9
beta_two = 0.999
BF = jnp.bfloat16
F32 = jnp.float32
NN = (((1,), (0,)), ((), ()))
NT = (((1,), (1,)), ((), ()))


def dot(a, b, dims=NN):
    return lax.dot_general(a, b, dims, preferred_element_type=F32)


def vmem(mib):
    return pltpu.CompilerParams(
        dimension_semantics=("arbitrary",), vmem_limit_bytes=mib * 1024 * 1024
    )


def flip(value, axis, bit):
    size = lax.axis_size(axis)
    return lax.ppermute(value, axis, [(i, i ^ bit) for i in range(size)])


def bits(size):
    out, bit = [], 1
    while bit < size:
        out.append(bit)
        bit *= 2
    return out


def gather_all(part, steps):
    held = part[None]
    for axis, bit in steps:
        held = jnp.concatenate([held, flip(held, axis, bit)], axis=0)
    return held


def reduce_all(parts, steps):
    held = parts
    for axis, bit in reversed(steps):
        half = held.shape[0] // 2
        came = flip(held[half:], axis, bit)
        held = (held[:half].astype(F32) + came.astype(F32)).astype(BF)
    return held[0]


def dp_order(steps):
    marks = [bit for axis, bit in steps if axis == "dp"]
    return [
        sum(bit for k, bit in enumerate(marks) if (j >> k) & 1) for j in range(2 ** len(marks))
    ]


def rows_at(order, j, my_dp, span):
    return pl.ds(pl.multiple_of((order[j] ^ my_dp) * span, span), span)


def head_mask(shape, head):
    lane = lax.broadcasted_iota(jnp.int32, shape, 1)
    return (lane < HEAD_DIM) if head == 0 else (lane >= HEAD_DIM)


def attend_kernel(
    order, ids, x_ref, w_ref, bias_ref, qf_ref, kf_ref, q_ref, k_ref, v_ref, ho_ref, lse_ref,
    w_all, keys, vals_t,
):
    my_dp = ids[2]
    span = w_ref.shape[2]
    for j in range(len(order)):
        w_all[rows_at(order, j, my_dp, span), :] = w_ref[j, 0]

    @pl.when(pl.program_id(0) == 0)
    def _():
        keys[:, PAIR:] = kf_ref[0]

    for t in range(LEN // TILE):
        at = slice(t * TILE, (t + 1) * TILE)
        got = dot(x_ref[0, at], w_all[...])
        q_ref[0, at] = (got[:, :PAIR] + bias_ref[0, 0:1]).astype(BF)
        key = got[:, PAIR : 2 * PAIR].astype(BF)
        k_ref[0, at] = key
        keys[at, :PAIR] = key
        val = (got[:, 2 * PAIR :] + bias_ref[0, 1:2]).astype(BF)
        v_ref[0, at] = val
        vals_t[:, at] = val.T

    for t in range(LEN // TILE):
        at = slice(t * TILE, (t + 1) * TILE)
        query = q_ref[0, at] * BF(0.125)
        mixed = []
        for head in range(2):
            mine = jnp.where(head_mask((TILE, PAIR), head), query, BF(0))
            wide = jnp.concatenate([mine, qf_ref[0, at]], axis=1)
            scores = dot(keys[...], wide, NT)
            top = jnp.max(scores, axis=0, keepdims=True)
            probs = jnp.exp(scores - top)
            total = jnp.sum(probs, axis=0, keepdims=True)
            lse_ref[0, head : head + 1, at] = top + jnp.log(total)
            out = dot(vals_t[head * HEAD_DIM : (head + 1) * HEAD_DIM, :], probs.astype(BF))
            mixed.append(out * (1.0 / total))
        ho_ref[at, :] = jnp.concatenate(mixed, axis=0).T.astype(BF)


def attend(ids, tokens, w_parts, bias, qf, kf, order):
    groups = w_parts.shape[1]
    n_dp, span = len(order), w_parts.shape[2]
    pair = pl.BlockSpec((1, LEN, PAIR), lambda g, ids: (g, 0, 0))
    feats = pl.BlockSpec((1, LEN, PAIR), lambda g, ids: (ids[0], 0, 0))
    return pl.pallas_call(
        functools.partial(attend_kernel, order),
        grid_spec=pltpu.PrefetchScalarGridSpec(
            num_scalar_prefetch=1,
            grid=(groups,),
            in_specs=[
                pl.BlockSpec((1, LEN, D), lambda g, ids: (ids[0], 0, 0)),
                pl.BlockSpec((n_dp, 1, span, 3 * PAIR), lambda g, ids: (0, g, 0, 0)),
                pl.BlockSpec((1, 2, PAIR), lambda g, ids: (g ^ ids[1], 0, 0)),
                feats,
                feats,
            ],
            out_specs=[
                pair,
                pair,
                pair,
                pl.BlockSpec((LEN, PAIR), lambda g, ids: (0, g ^ ids[1])),
                pl.BlockSpec((1, 2, LEN), lambda g, ids: (g, 0, 0)),
            ],
            scratch_shapes=[
                pltpu.VMEM((D, 3 * PAIR), BF),
                pltpu.VMEM((LEN, 2 * PAIR), BF),
                pltpu.VMEM((PAIR, LEN), BF),
            ],
        ),
        out_shape=[
            jax.ShapeDtypeStruct((groups, LEN, PAIR), BF),
            jax.ShapeDtypeStruct((groups, LEN, PAIR), BF),
            jax.ShapeDtypeStruct((groups, LEN, PAIR), BF),
            jax.ShapeDtypeStruct((LEN, D), BF),
            jax.ShapeDtypeStruct((groups, 2, LEN), F32),
        ],
        compiler_params=vmem(48),
        cost_estimate=pl.CostEstimate(
            flops=10_000_000_000, bytes_accessed=8_000_000, transcendentals=8_400_000
        ),
        name="attend",
    )(ids, tokens, w_parts, bias, qf, kf)


def norm_stats(value):
    center = value - jnp.mean(value, axis=-1, keepdims=True)
    spread = jnp.mean(center * center, axis=-1, keepdims=True)
    inverse = lax.rsqrt(spread + 1e-05)
    return center * inverse, inverse


def norm_backward(upstream, normal, inverse, gain):
    scaled = upstream * gain
    return inverse * (
        scaled
        - jnp.mean(scaled, axis=-1, keepdims=True)
        - normal * jnp.mean(scaled * normal, axis=-1, keepdims=True)
    )


def tokenwise_kernel(
    order_a, order_b, keep, ids, x_ref, ho_ref, cot_ref, wa_ref, wb_ref, par_ref, ffb_ref, *rest
):
    if keep:
        (out_ref, gatt_ref, gh_ref, hid_ref, gpre_ref, low_ref, sums_ref, ffs_ref,
         w_out, w_up, w_down, slope, acc) = rest
    else:
        (out_ref, gatt_ref, gh_ref, w_out, w_up, w_down, slope, hid_ref) = rest
    my_mp, my_dp = ids[1], ids[2]
    step = pl.program_id(0)
    span = wa_ref.shape[2]
    groups = wa_ref.shape[1]
    wide = FF // groups

    @pl.when(step == 0)
    def _():
        for g in range(groups):
            col = g ^ my_mp
            narrow_at = pl.ds(pl.multiple_of(col * PAIR, PAIR), PAIR)
            wide_at = pl.ds(pl.multiple_of(col * wide, wide), wide)
            for j in range(len(order_a)):
                row = rows_at(order_a, j, my_dp, span)
                w_out[row, narrow_at] = wa_ref[j, g, :, :PAIR]
                w_up[row, wide_at] = wa_ref[j, g, :, PAIR:]
            for j in range(len(order_b)):
                w_down[rows_at(order_b, j, my_dp, span), wide_at] = wb_ref[j, g]

    gain_one, gain_two = par_ref[0:1], par_ref[1:2]
    shift_att, shift_ffn, shift_one, shift_two = (par_ref[k : k + 1] for k in range(2, 6))
    attention = dot(ho_ref[...], w_out[...], NT) + shift_att
    normal_one, inverse_one = norm_stats(x_ref[0].astype(F32) + attention)
    normed = normal_one * gain_one + shift_one
    normed_low = normed.astype(BF)
    branch = shift_ffn
    chunk = 512
    for c in range(FF // chunk):
        at = slice(c * chunk, (c + 1) * chunk)
        pre = dot(normed_low, w_up[:, at]) + ffb_ref[:, at]
        phi = 0.5 * (1.0 + lax.erf(pre * 0.7071067811865476))
        hidden = (pre * phi).astype(BF)
        hid_ref[:, at] = hidden
        slope[:, at] = phi + pre * jnp.exp(-0.5 * pre * pre) * 0.3989422804014327
        branch = branch + dot(hidden, w_down[:, at], NT)
    normal_two, inverse_two = norm_stats(normed + branch)
    out_ref[...] = (normal_two * gain_two + shift_two).astype(BF)
    upstream = cot_ref[0].astype(F32)
    g_final = norm_backward(upstream, normal_two, inverse_two, gain_two)
    g_final_low = g_final.astype(BF)
    g_normed = g_final
    for c in range(FF // chunk):
        at = slice(c * chunk, (c + 1) * chunk)
        g_pre = (dot(g_final_low, w_down[:, at]) * slope[:, at]).astype(BF)
        if keep:
            gpre_ref[:, at] = g_pre
            here = jnp.sum(g_pre.astype(F32), axis=0, keepdims=True)

            @pl.when(step == 0)
            def _(at=at, here=here):
                ffs_ref[:, at] = here

            @pl.when(step > 0)
            def _(at=at, here=here):
                ffs_ref[:, at] += here

        g_normed = g_normed + dot(g_pre, w_up[:, at], NT)
    g_attention = norm_backward(g_normed, normal_one, inverse_one, gain_one)
    g_attention_low = g_attention.astype(BF)
    gatt_ref[...] = g_attention
    gh_ref[...] = dot(g_attention_low, w_out[...]).astype(BF)
    if keep:
        low_ref[0] = normed_low
        low_ref[1] = g_final_low
        low_ref[2] = g_attention_low
        terms = (g_normed * normal_one, upstream * normal_two, g_attention, g_final, g_normed, upstream)
        for k, term in enumerate(terms):
            part = jnp.sum(term.reshape(TILE // 8, 8, D), axis=0)

            @pl.when(step == 0)
            def _(k=k, part=part):
                acc[k] = part

            @pl.when(step > 0)
            def _(k=k, part=part):
                acc[k] += part

        @pl.when(step == pl.num_programs(0) - 1)
        def _():
            for k in range(6):
                sums_ref[k : k + 1] = jnp.sum(acc[k], axis=0, keepdims=True)


def tokenwise(ids, tokens, heads_out, cotangent, wa, wb, params, ff_shift, order_a, order_b, keep):
    full = lambda shape: pl.BlockSpec(shape, lambda t, ids: (0,) * len(shape))
    row = pl.BlockSpec((1, TILE, D), lambda t, ids: (ids[0], t, 0))
    flat = pl.BlockSpec((TILE, D), lambda t, ids: (t, 0))
    broad = pl.BlockSpec((TILE, FF), lambda t, ids: (t, 0))
    out_specs = [flat, flat, flat]
    out_shape = [
        jax.ShapeDtypeStruct((LEN, D), BF),
        jax.ShapeDtypeStruct((LEN, D), F32),
        jax.ShapeDtypeStruct((LEN, D), BF),
    ]
    scratch = [
        pltpu.VMEM((D, D), BF),
        pltpu.VMEM((D, FF), BF),
        pltpu.VMEM((D, FF), BF),
        pltpu.VMEM((TILE, FF), F32),
    ]
    if keep:
        out_specs += [broad, broad, pl.BlockSpec((3, TILE, D), lambda t, ids: (0, t, 0)), full((6, D)), full((1, FF))]
        out_shape += [
            jax.ShapeDtypeStruct((LEN, FF), BF),
            jax.ShapeDtypeStruct((LEN, FF), BF),
            jax.ShapeDtypeStruct((3, LEN, D), BF),
            jax.ShapeDtypeStruct((6, D), F32),
            jax.ShapeDtypeStruct((1, FF), F32),
        ]
        scratch += [pltpu.VMEM((6, 8, D), F32)]
    else:
        scratch += [pltpu.VMEM((TILE, FF), BF)]
    return pl.pallas_call(
        functools.partial(tokenwise_kernel, order_a, order_b, keep),
        grid_spec=pltpu.PrefetchScalarGridSpec(
            num_scalar_prefetch=1,
            grid=(LEN // TILE,),
            in_specs=[row, flat, row, full(wa.shape), full(wb.shape), full((6, D)), full((1, FF))],
            out_specs=out_specs,
            scratch_shapes=scratch,
        ),
        out_shape=out_shape,
        compiler_params=vmem(48),
        cost_estimate=pl.CostEstimate(
            flops=14_000_000_000, bytes_accessed=20_000_000, transcendentals=4_200_000
        ),
        name="tokenwise_keep" if keep else "tokenwise",
    )(ids, tokens, heads_out, cotangent, wa, wb, params, ff_shift)


def turned(source, order, my_dp, tall, tmp):
    tmp[...] = source.T
    span = D // len(order)
    for j in range(len(order)):
        tall[j * span : (j + 1) * span, :] = tmp[rows_at(order, j, my_dp, span), :]


def weight_kernel(order_a, order_b, ids, low_ref, ho_ref, hid_ref, gpre_ref, ga_ref, gb_ref, up_t, down_t, att_t, tmp):
    my_dp = ids[2]

    @pl.when(pl.program_id(0) == 0)
    def _():
        turned(low_ref[0], order_a, my_dp, up_t, tmp)
        turned(low_ref[1], order_b, my_dp, down_t, tmp)
        turned(low_ref[2], order_a, my_dp, att_t, tmp)

    n_a, n_b = len(order_a), len(order_b)
    ga_ref[:, 0, :, :PAIR] = dot(att_t[...], ho_ref[...]).astype(BF).reshape(n_a, D // n_a, PAIR)
    wide = gpre_ref.shape[1]
    ga_ref[:, 0, :, PAIR:] = dot(up_t[...], gpre_ref[...]).astype(BF).reshape(n_a, D // n_a, wide)
    gb_ref[:, 0] = dot(down_t[...], hid_ref[...]).astype(BF).reshape(n_b, D // n_b, wide)


def weight_grads(ids, lows, heads_out, hidden, g_pre, groups, order_a, order_b):
    wide = FF // groups
    n_a, n_b = len(order_a), len(order_b)
    broad = pl.BlockSpec((LEN, wide), lambda g, ids: (0, g ^ ids[1]))
    return pl.pallas_call(
        functools.partial(weight_kernel, order_a, order_b),
        grid_spec=pltpu.PrefetchScalarGridSpec(
            num_scalar_prefetch=1,
            grid=(groups,),
            in_specs=[
                pl.BlockSpec((3, LEN, D), lambda g, ids: (0, 0, 0)),
                pl.BlockSpec((LEN, PAIR), lambda g, ids: (0, g ^ ids[1])),
                broad,
                broad,
            ],
            out_specs=[
                pl.BlockSpec((n_a, 1, D // n_a, PAIR + wide), lambda g, ids: (0, g, 0, 0)),
                pl.BlockSpec((n_b, 1, D // n_b, wide), lambda g, ids: (0, g, 0, 0)),
            ],
            scratch_shapes=[pltpu.VMEM((D, LEN), BF)] * 4,
        ),
        out_shape=[
            jax.ShapeDtypeStruct((n_a, groups, D // n_a, PAIR + wide), BF),
            jax.ShapeDtypeStruct((n_b, groups, D // n_b, wide), BF),
        ],
        compiler_params=vmem(48),
        cost_estimate=pl.CostEstimate(
            flops=5_000_000_000, bytes_accessed=17_000_000, transcendentals=0
        ),
        name="weight_grads",
    )(ids, lows, heads_out, hidden, g_pre)


def attend_back_kernel(
    order, keep, ids, x_ref, w_ref, qf_ref, kf_ref, q_ref, k_ref, v_ref, ho_ref, lse_ref, gh_ref, gatt_ref, *rest
):
    if keep:
        (tg_ref, gw_ref, gb_ref, w_all, keys, keys_t, delta, dk, dv, grads, x_t, tmp) = rest
    else:
        (tg_ref, w_all, keys, keys_t, delta, dk, dv, grads) = rest
    my_dp = ids[2]
    span = w_ref.shape[2]
    for j in range(len(order)):
        w_all[rows_at(order, j, my_dp, span), :] = w_ref[j, 0]

    @pl.when(pl.program_id(0) == 0)
    def _():
        keys[:, PAIR:] = kf_ref[0]
        tg_ref[...] = gatt_ref[...]
        if keep:
            turned(x_ref[0], order, my_dp, x_t, tmp)

    keys[:, :PAIR] = k_ref[0]
    keys_t[...] = k_ref[0].T
    prod = (gh_ref[...].astype(F32) * ho_ref[...].astype(F32)).T
    delta[0:1] = jnp.sum(prod[:HEAD_DIM], axis=0, keepdims=True)
    delta[1:2] = jnp.sum(prod[HEAD_DIM:], axis=0, keepdims=True)
    dk[...] = jnp.zeros_like(dk)
    dv[...] = jnp.zeros_like(dv)
    for t in range(LEN // TILE):
        at = slice(t * TILE, (t + 1) * TILE)
        query, back = q_ref[0, at], gh_ref[at, :]
        d_query = []
        for head in range(2):
            mask = head_mask((TILE, PAIR), head)
            mine = jnp.where(mask, query, BF(0))
            wide = jnp.concatenate([mine * BF(0.125), qf_ref[0, at]], axis=1)
            own_back = jnp.where(mask, back, BF(0))
            lse, row = lse_ref[0, head : head + 1, at], delta[head : head + 1, at]
            total = None
            for s in range(LEN // TILE):
                kat = slice(s * TILE, (s + 1) * TILE)
                probs = jnp.exp(dot(keys[kat, :], wide, NT) - lse)
                g_probs = dot(v_ref[0, kat], own_back, NT)
                g_raw = (probs * (g_probs - row)).astype(BF)
                dv[kat, :] += dot(probs.astype(BF), own_back)
                dk[kat, :] += dot(g_raw, mine)
                part = dot(keys_t[head * HEAD_DIM : (head + 1) * HEAD_DIM, kat], g_raw)
                total = part if total is None else total + part
            d_query.append(total)
        grads[at, :PAIR] = (jnp.concatenate(d_query, axis=0).T * 0.125).astype(BF)
    grads[:, PAIR : 2 * PAIR] = (dk[...] * 0.125).astype(BF)
    grads[:, 2 * PAIR :] = dv[...].astype(BF)
    for t in range(LEN // TILE):
        at = slice(t * TILE, (t + 1) * TILE)
        tg_ref[at, :] += dot(grads[at, :], w_all[...], NT)
    if keep:
        n = len(order)
        gw_ref[:, 0] = dot(x_t[...], grads[...]).astype(BF).reshape(n, D // n, 3 * PAIR)
        gb_ref[0, 0:1] = jnp.sum(grads[:, :PAIR].astype(F32), axis=0, keepdims=True)
        gb_ref[0, 1:2] = jnp.sum(grads[:, 2 * PAIR :].astype(F32), axis=0, keepdims=True)


def attend_back(ids, tokens, w_parts, qf, kf, q, k, v, heads_out, lse, g_heads, g_att, order, keep):
    groups = w_parts.shape[1]
    n_dp, span = len(order), w_parts.shape[2]
    pair = pl.BlockSpec((1, LEN, PAIR), lambda g, ids: (g, 0, 0))
    feats = pl.BlockSpec((1, LEN, PAIR), lambda g, ids: (ids[0], 0, 0))
    column = pl.BlockSpec((LEN, PAIR), lambda g, ids: (0, g ^ ids[1]))
    full = pl.BlockSpec((LEN, D), lambda g, ids: (0, 0))
    part = pl.BlockSpec((n_dp, 1, span, 3 * PAIR), lambda g, ids: (0, g, 0, 0))
    out_specs, out_shape = [full], [jax.ShapeDtypeStruct((LEN, D), F32)]
    scratch = [
        pltpu.VMEM((D, 3 * PAIR), BF),
        pltpu.VMEM((LEN, 2 * PAIR), BF),
        pltpu.VMEM((PAIR, LEN), BF),
        pltpu.VMEM((2, LEN), F32),
        pltpu.VMEM((LEN, PAIR), F32),
        pltpu.VMEM((LEN, PAIR), F32),
        pltpu.VMEM((LEN, 3 * PAIR), BF),
    ]
    if keep:
        out_specs += [part, pl.BlockSpec((1, 2, PAIR), lambda g, ids: (g ^ ids[1], 0, 0))]
        out_shape += [
            jax.ShapeDtypeStruct((n_dp, groups, span, 3 * PAIR), BF),
            jax.ShapeDtypeStruct((groups, 2, PAIR), F32),
        ]
        scratch += [pltpu.VMEM((D, LEN), BF)] * 2
    return pl.pallas_call(
        functools.partial(attend_back_kernel, order, keep),
        grid_spec=pltpu.PrefetchScalarGridSpec(
            num_scalar_prefetch=1,
            grid=(groups,),
            in_specs=[
                pl.BlockSpec((1, LEN, D), lambda g, ids: (ids[0], 0, 0)),
                part,
                feats,
                feats,
                pair,
                pair,
                pair,
                column,
                pl.BlockSpec((1, 2, LEN), lambda g, ids: (g, 0, 0)),
                column,
                full,
            ],
            out_specs=out_specs,
            scratch_shapes=scratch,
        ),
        out_shape=out_shape,
        compiler_params=vmem(48),
        cost_estimate=pl.CostEstimate(
            flops=20_000_000_000, bytes_accessed=12_000_000, transcendentals=8_400_000
        ),
        name="attend_back_keep" if keep else "attend_back",
    )(ids, tokens, w_parts, qf, kf, q, k, v, heads_out, lse, g_heads, g_att)


def adam_step(weight, grad_sum, first, second, rate, decay):
    first_new = beta_one * first + (1.0 - beta_one) * grad_sum
    second_new = beta_two * second + (1.0 - beta_two) * grad_sum * grad_sum
    first_hat = first_new / (1.0 - beta_one**STEP)
    second_hat = second_new / (1.0 - beta_two**STEP)
    weight_new = weight - rate * (first_hat / (jnp.sqrt(second_hat) + 1e-08) + decay * weight)
    return (weight_new, first_new, second_new)


def features(segment_ids, pad_lengths):
    place = jnp.arange(LEN, dtype=jnp.int32)[None, :, None]
    lane = jnp.arange(PAIR, dtype=jnp.int32)[None, None, :]
    segment = segment_ids[:, :, None]
    padding = place >= (LEN - pad_lengths)[:, None, None]
    high, low = place // 32, place % 32
    hit = (
        ((lane < 4) & (lane == segment))
        | ((lane >= 4) & (lane < 36) & (lane - 4 == high))
        | ((lane >= 36) & (lane < 68) & (lane - 36 == low))
    )
    counts = jnp.where(padding, (lane >= 4) & (lane < 68), lane < 4)
    qf = jnp.where(hit, -FAR, 0.0).astype(BF)
    kf = jnp.where(counts & ~hit, 1.0, 0.0).astype(BF)
    return qf, kf


def per_device(
    tokens, segment_ids, pad_lengths, cotangent,
    w_qkv, w_out, w_up, w_down, qv_bias, ff_bias, norm_gains, norm_shifts,
    first_qkv, first_out, first_up, first_down, first_qv_bias, first_ff_bias, first_gains, first_shifts,
    second_qkv, second_out, second_up, second_down, second_qv_bias, second_ff_bias, second_gains, second_shifts,
):
    n_dp, n_mp = lax.axis_size("dp"), lax.axis_size("mp")
    my_dp, my_mp = lax.axis_index("dp"), lax.axis_index("mp")
    mp_steps = [("mp", bit) for bit in bits(n_mp)]
    near, *far = [("dp", bit) for bit in bits(n_dp)]
    steps_a = mp_steps + far + [near]
    steps_b = mp_steps + far[::-1] + [near]
    order_a, order_b = dp_order(steps_a), dp_order(steps_b)
    span = D // n_dp

    part_qkv = w_qkv.astype(BF).reshape(span, 3 * PAIR)
    part_a = jnp.concatenate([w_out.T, w_up], axis=1).astype(BF)
    part_b = w_down.T.astype(BF)
    small = jnp.concatenate(
        [qv_bias.reshape(-1), ff_bias.reshape(-1), norm_gains.reshape(-1), norm_shifts.reshape(-1)]
    ).astype(BF)
    small_all = lax.all_gather(lax.all_gather(small, "dp", axis=0), "mp", axis=0).astype(F32)
    all_qkv = gather_all(part_qkv, steps_a).reshape(n_dp, n_mp, span, 3 * PAIR)
    all_a = gather_all(part_a, steps_a).reshape(n_dp, n_mp, span, -1)
    all_b = gather_all(part_b, steps_b).reshape(n_dp, n_mp, span, -1)

    cuts = [qv_bias.size, ff_bias.size, norm_gains.size, norm_shifts.size]
    ends = [sum(cuts[: k + 1]) for k in range(4)]
    bias_rows = (
        small_all[:, :, : ends[0]]
        .reshape(n_mp, n_dp, 2, 2, HEAD_DIM // n_dp)
        .transpose(0, 2, 3, 1, 4)
        .reshape(n_mp, 2, PAIR)
    )
    ff_shift = (
        small_all[:, :, ends[0] : ends[1]]
        .reshape(n_mp, n_dp, FF // HEAD_DIM // n_mp, HEAD_DIM // n_dp)
        .transpose(0, 2, 1, 3)
        .reshape(1, FF)
    )
    params = (
        small_all[0, :, ends[1] :]
        .reshape(n_dp, 6, span)
        .transpose(1, 0, 2)
        .reshape(6, D)
    )
    qf, kf = features(segment_ids, pad_lengths)

    def ids_of(row):
        return jnp.stack([row, my_mp, my_dp]).astype(jnp.int32)

    mine, other = ids_of(my_mp), ids_of(my_mp ^ 1)
    q, k, v, heads_out, lse = attend(mine, tokens, all_qkv, bias_rows, qf, kf, order_a)
    own_out, g_att, g_heads, hidden, g_pre, lows, sums, ff_sums = tokenwise(
        mine, tokens, heads_out, cotangent, all_a, all_b, params, ff_shift, order_a, order_b, True
    )
    grad_a, grad_b = weight_grads(mine, lows, heads_out, hidden, g_pre, n_mp, order_a, order_b)
    own_grad, grad_qkv, bias_sums = attend_back(
        mine, tokens, all_qkv, qf, kf, q, k, v, heads_out, lse, g_heads, g_att, order_a, True
    )
    q2, k2, v2, heads_out2, lse2 = attend(other, tokens, all_qkv, bias_rows, qf, kf, order_a)
    other_out, g_att2, g_heads2 = tokenwise(
        other, tokens, heads_out2, cotangent, all_a, all_b, params, ff_shift, order_a, order_b, False
    )
    (other_grad,) = attend_back(
        other, tokens, all_qkv, qf, kf, q2, k2, v2, heads_out2, lse2, g_heads2, g_att2, order_a, False
    )

    middle = (my_mp == 1) | (my_mp == 2)

    def spread(own):
        close = lax.ppermute(own, "mp", [(1, 2), (2, 1)])
        distant = lax.ppermute(own, "mp", [(3, 1), (0, 2)])
        close_on = lax.ppermute(close, "mp", [(1, 0), (2, 3)])
        distant_on = lax.ppermute(distant, "mp", [(1, 0), (2, 3)])
        return jnp.where(middle, close, close_on), jnp.where(middle, distant, distant_on)

    lower = my_mp < 2

    def place(own, other, close, distant):
        even = (my_mp % 2) == 0
        first, second = jnp.where(even, own, other), jnp.where(even, other, own)
        return jnp.stack(
            [
                jnp.where(lower, first, distant),
                jnp.where(lower, second, close),
                jnp.where(lower, close, first),
                jnp.where(lower, distant, second),
            ]
        )

    layer_out = place(own_out, other_out, *spread(own_out))
    close, distant = spread(own_grad.astype(BF))
    tokens_grad = place(own_grad, other_grad, close.astype(F32), distant.astype(F32))

    sum_a = reduce_all(grad_a.reshape(n_dp * n_mp, span, -1), steps_a).astype(F32)
    sum_b = reduce_all(grad_b.reshape(n_dp * n_mp, span, -1), steps_b).astype(F32)
    sum_qkv = reduce_all(grad_qkv.reshape(n_dp * n_mp, span, 3 * PAIR), steps_a).astype(F32)
    small_sum = lax.psum(
        jnp.concatenate([bias_sums.reshape(-1), ff_sums.reshape(-1), sums.reshape(-1)]),
        ("dp", "mp"),
    )
    at_bias = small_sum[: 2 * D].reshape(n_mp, 2, 2, n_dp, HEAD_DIM // n_dp)
    at_ff = small_sum[2 * D : 2 * D + FF].reshape(n_mp, FF // HEAD_DIM // n_mp, n_dp, HEAD_DIM // n_dp)
    at_norm = small_sum[2 * D + FF :].reshape(6, n_dp, span)
    pick = lambda a, axis, index: lax.dynamic_index_in_dim(a, index, axis, keepdims=False)
    norm_mine = pick(at_norm, 1, my_dp)
    final_grads = (
        sum_qkv.reshape(w_qkv.shape),
        sum_a[:, :PAIR].T,
        sum_a[:, PAIR:],
        sum_b.T,
        pick(pick(at_bias, 0, my_mp), 2, my_dp),
        pick(pick(at_ff, 0, my_mp), 1, my_dp),
        norm_mine[:2],
        norm_mine[2:],
    )
    masters = (w_qkv, w_out, w_up, w_down, qv_bias, ff_bias, norm_gains, norm_shifts)
    step_rates = (D ** (-0.5), (D // 64) ** (-0.5), D ** (-0.5), FF ** (-0.5), 0.3, 0.3, 0.3, 0.3)
    decays = (0.01, 0.01, 0.01, 0.01, 0.0, 0.0, 0.0, 0.0)
    firsts = (first_qkv, first_out, first_up, first_down, first_qv_bias, first_ff_bias, first_gains, first_shifts)
    seconds = (second_qkv, second_out, second_up, second_down, second_qv_bias, second_ff_bias, second_gains, second_shifts)
    updated = [
        adam_step(masters[s], final_grads[s], firsts[s], seconds[s], step_rates[s], decays[s])
        for s in range(8)
    ]
    return tuple(
        [layer_out, tokens_grad]
        + [entry[0] for entry in updated]
        + [entry[1] for entry in updated]
        + [entry[2] for entry in updated]
    )


def solution(mesh):
    weights = (
        P("dp", None, "mp"),
        P("mp", "dp"),
        P("dp", "mp"),
        P("mp", "dp"),
        P(None, "mp", "dp"),
        P("mp", "dp"),
        P(None, "dp"),
        P(None, "dp"),
    )
    rows = P("dp", None, None)
    return jax.shard_map(
        per_device,
        mesh=mesh,
        in_specs=(rows, P("dp", None), P("dp"), rows) + weights * 3,
        out_specs=(rows, rows) + weights * 3,
        check_vma=False,
    )
```

time: 1660 us -> 521 us (0.31)
  waiting for transfers between devices: 1040 us -> 119 us
  matrix products: 315 us -> 0 us
  Pallas kernels: 0 us -> 194 us
  other arithmetic: 113 us -> 37.7 us
  starting transfers between devices: 1.05 us -> 64.5 us
  blocking collectives: 88.7 us -> 59.4 us
  local copies, waits for them, and re-layouts: 57.8 us -> 35.1 us
  loops' own time: 17 us -> 0 us
    psum x4 -> x0, waiting for transfers between devices: 960 us -> none  [the longest x1 286 us: per_device(): branch = lax.psum(ffn_part, 'mp') + shift_rows[1]]
    dot_general x52 -> x0, matrix products: 315 us -> none  [the longest x4 94.4 us: backward_block(): jnp.einsum('shqk,sqhd->skhd', g_raw, block_q, preferred_element_type=jnp....]
    pallas_call x0 -> x7, Pallas kernels: none -> 194 us  [the longest x2 74.3 us: attend_back(): pl.pallas_call(functools.partial(attend_back_kernel, order, keep), grid_s...]
    ppermute x0 -> x38, waiting for transfers between devices: none -> 119 us  [the longest x30 119 us: flip(): return lax.ppermute(value, axis, [(i, i ^ bit) for i in range(size)])]
    reduce_scatter x4 -> x0, waiting for transfers between devices: 71.6 us -> none  [the longest x1 37.1 us: per_device(): lax.psum_scatter(summed[0], 'dp', scatter_dimension=0, tiled=True)]
    ppermute x0 -> x38, starting transfers between devices: none -> 64.5 us  [the longest x30 45.9 us: flip(): return lax.ppermute(value, axis, [(i, i ^ bit) for i in range(size)])]
    reduce_sum x18 -> x0, other arithmetic: 54.8 us -> none  [the longest x2 12.3 us: norm_forward(): center = value - jnp.mean(value, axis=-1, keepdims=True)]
    all_gather x8 -> x2, blocking collectives: 74.9 us -> 22.2 us  [the longest x1 13.3 us: per_device(): lax.all_gather(lax.all_gather(small, 'dp', axis=0), 'mp', axis=0)]
  transfers between devices with their start and end apart: 10 -> 38, of which waited for: 7 -> 18; matrix products, arithmetic and copies ran while one was open for 20% -> 10% of each run, Pallas kernels for 0% -> 25%
where the time goes in v1:
time: 521 us; the launch traced here: 513 us
  Pallas kernels  194 us (37%)
  waiting for transfers between devices  119 us (23%)
  starting transfers between devices  64.5 us (12%)
  blocking collectives  59.4 us (11%)
  other arithmetic  37.7 us (7%)
  local copies, waits for them, and re-layouts  35.1 us (7%)
    ppermute x30, waiting for transfers between devices, flip(): return lax.ppermute(value, axis, [(i, i ^ bit) for i in range(size)])  119 us
    pallas_call x2, Pallas kernels, attend_back(): pl.pallas_call(functools.partial(attend_back_kernel, order, keep), grid_s...  74.3 us
    pallas_call x2, Pallas kernels, attend(): pl.pallas_call(functools.partial(attend_kernel, order), grid_spec=pltpu.P...  59.9 us
    pallas_call x2, Pallas kernels, tokenwise(): pl.pallas_call(functools.partial(tokenwise_kernel, order_a, order_b, keep...  49.4 us
    ppermute x30, starting transfers between devices, flip(): return lax.ppermute(value, axis, [(i, i ^ bit) for i in range(size)])  45.9 us
    psum x1, blocking collectives, per_device(): lax.psum(jnp.concatenate([bias_sums.reshape(-1), ff_sums.reshape(-1), sum...  37.2 us
    unnamed x136, local copies, waits for them, and re-layouts  22.7 us
    all_gather x1, blocking collectives, per_device(): lax.all_gather(lax.all_gather(small, 'dp', axis=0), 'mp', axis=0)  13.3 us
  transfers between devices with their start and end apart: 38, of which 18 were waited for; matrix products, arithmetic and copies ran while one was open for 10% of the time, Pallas kernels for 25%

profile of v1, /device:TPU:0, one launch (start us, length us, event | category | flops | bytes accessed | tf_op | source)
XLA Modules:
  0.0 512.6 jit_solution(14844917119105587324)
XLA Ops:
  1.7 3.1 collective-permute-start
  8.7 2.0 collective-permute-start.5
  15.9 8.9 %all-gather.1 = bf16[8,1,480]{2,1,0:T(2,128)(2,1)S(1)} all-gather(bf16[1,1,480]{2,1,0:T(2,128)(2,1)S(1)} %maximum_bitcast_fusion), channel_id=1, replica_groups=mesh['dp'=8,'mp'=4] {'dp'}, dimensions={0}, use_global_device_ids=true | all-gather | bytes 8640 | tf_op jit(solution)/shard_map/all_gather | solution.py:541
  24.8 13.3 %all-gather = bf16[32,480]{1,0:T(8,128)(2,1)S(1)} all-gather(bf16[8,480]{1,0:T(8,128)(2,1)S(1)} %bitcast.105), channel_id=2, replica_groups=mesh['dp'=8,'mp'=4] {'mp'}, dimensions={0}, use_global_device_ids=true | all-gather | bytes 38400 | tf_op jit(solution)/shard_map/all_gather | solution.py:541
  38.6 3.5 select_convert_fusion
  44.3 2.4 collective-permute-start.11
  48.1 8.3 %collective-permute-done.1 = bf16[2,64,384]{2,1,0:T(8,128)(2,1)S(1)} collective-permute-done((bf16[2,64,384]{2,1,0:T(8,128)(2,1)S(1)}, bf16[2,64,384]{2,1,0:T(8,128)(2,1)S(1)}, u32[]{:S(2)}, u32[]{:S(2)}) %collective-permute-start.1) | collective-permute-done | bytes 98336 | tf_op jit(solution)/shard_map/ppermute | solution.py:40
  59.0 1.6 collective-permute-start.12
  62.6 1.6 collective-permute-start.3
  64.3 3.6 collective-permute-done.12
  68.0 1.8 collective-permute-start.13
  69.9 1.7 collective-permute-done.7
  73.1 3.3 collective-permute-done.3
  81.6 6.3 %collective-permute-done.8 = bf16[8,64,640]{2,1,0:T(8,128)(2,1)S(1)} collective-permute-done((bf16[8,64,640]{2,1,0:T(8,128)(2,1)S(1)}, bf16[8,64,640]{2,1,0:T(8,128)(2,1)S(1)}, u32[]{:S(2)}, u32[]{:S(2)}) %collective-permute-start.8) | collective-permute-done | bytes 655392 | tf_op jit(solution)/shard_map/ppermute | solution.py:40
  90.4 29.6 %attend.3 = (bf16[4,1024,128]{2,1,0:T(8,128)(2,1)S(1)}, bf16[4,1024,128]{2,1,0:T(8,128)(2,1)S(1)}, bf16[4,1024,128]{2,1,0:T(8,128)(2,1)S(1)}, bf16[1024,512]{1,0:T(8,128)(2,1)S(1)}, f32[4,2,1024]{2,1,0:T(2,128)S(1)}) custom-call(s32[3]{0:T(128)S(1)} %add_add_fusion.1.ids, bf16[4,1024,512]{2,1,0:T(8,128)(2,1)} %x_ref.11, bf16[8,4,64,384]{3,2,1,0:T(8,128)(2,1)} %bitcast.114, ...), custom_call_target="tpu_custom_call" | custom-call | flops 10000000000 | bytes 8000000 | tf_op jit(solution)/shard_map/attend/pallas_call | solution.py:129
  123.0 30.2 %attend.2 = (bf16[4,1024,128]{2,1,0:T(8,128)(2,1)S(1)}, bf16[4,1024,128]{2,1,0:T(8,128)(2,1)S(1)}, bf16[4,1024,128]{2,1,0:T(8,128)(2,1)S(1)}, bf16[1024,512]{1,0:T(8,128)(2,1)S(1)}, f32[4,2,1024]{2,1,0:T(2,128)S(1)}) custom-call(s32[3]{0:T(128)S(1)} %add_add_fusion.ids, bf16[4,1024,512]{2,1,0:T(8,128)(2,1)} %x_ref.11, bf16[8,4,64,384]{3,2,1,0:T(8,128)(2,1)} %bitcast.115, ...), custom_call_target="tpu_custom_call" | custom-call | flops 10000000000 | bytes 8000000 | tf_op jit(solution)/shard_map/attend/pallas_call | solution.py:129
  156.7 27.6 %tokenwise_keep.1 = (bf16[1024,512]{1,0:T(8,128)(2,1)S(1)}, f32[1024,512]{1,0:T(8,128)S(1)}, bf16[1024,512]{1,0:T(8,128)(2,1)S(1)}, bf16[1024,2048]{1,0:T(8,128)...) custom-call(s32[3]{0:T(128)S(1)} %add_add_fusion.ids, ...), custom_call_target="tpu_custom_call" | custom-call | flops 14000000000 | bytes 20000000 | tf_op jit(solution)/shard_map/tokenwise_keep/pallas_call | solution.py:305
  191.3 38.2 %attend_back_keep.1 = (f32[1024,512]{1,0:T(8,128)}, bf16[8,4,64,384]{3,2,1,0:T(8,128)(2,1)}, f32[4,2,128]{2,1,0:T(2,128)S(1)}) custom-call(s32[3]{0:T(128)S(1)} %add_add_fusion.ids, bf16[4,1024,512]{2,1,0:T(8,128)(2,1)} %x_ref.11, bf16[8,4,64,384]{3,2,1,0:T(8,128)(2,1)} %bitcast.116, bf16[4,1024,128]{2,1,0:T(8,128)(2,1)S(1)} %get-tuple-element.183.qf_ref, ...), custom_call_target="tpu_custom_call" | custom-call | flops 20000000000 | bytes 12000000 | tf_op jit(solution)/shard_map/attend_back_keep/pallas_call | solution.py:464
  229.5 37.2 %psum.7 = f32[6144]{0:T(1024)S(1)} all-reduce(f32[6144]{0:T(1024)S(1)} %pad_maximum_fusion.12), channel_id=1, replica_groups=mesh['dp'=8,'mp'=4] {'dp','mp'}, use_global_device_ids=true, to_apply=%region_0.1 | all-reduce | flops 6144 | bytes 49152 | tf_op jit(solution)/shard_map/psum | solution.py:618
  266.7 2.7 convert_element_type.210
  269.4 1.6 collective-permute-start.21
  271.1 7.5 %collective-permute-start.19 = (bf16[1024,512]{1,0:T(8,128)(2,1)}, bf16[1024,512]{1,0:T(8,128)(2,1)}, u32[]{:S(2)}, u32[]{:S(2)}) collective-permute-start(bf16[1024,512]{1,0:T(8,128)(2,1)} %convert_element_type.210), channel_id=1, source_target_pairs={{3,1},{0,2},{7,5},{4,6},{11,9},{8,10},{15,13},{12,14},{19,17},{16,... | collective-permute-start | bytes 3145736 | tf_op jit(solution)/shard_map/ppermute | solution.py:592
  278.5 21.8 %tokenwise.1 = (bf16[1024,512]{1,0:T(8,128)(2,1)S(1)}, f32[1024,512]{1,0:T(8,128)S(1)}, bf16[1024,512]{1,0:T(8,128)(2,1)S(1)}) custom-call(s32[3]{0:T(128)S(1)} %add_add_fusion.1.ids, bf16[4,1024,512]{2,1,0:T(8,128)(2,1)} %x_ref.11, bf16[1024,512]{1,0:T(8,128)(2,1)S(1)} %copy-done.18, bf16[4,1024,512]{2,1,0:T(8,128)(2,1)} %cot_ref.3, ...), custom_call_target="tpu_custom_call" | custom-call | flops 14000000000 | bytes 20000000 | tf_op jit(solution)/shard_map/tokenwise/pallas_call | solution.py:305
  303.5 10.9 %weight_grads.1 = (bf16[8,4,64,640]{3,2,1,0:T(8,128)(2,1)S(1)}, bf16[8,4,64,512]{3,2,1,0:T(8,128)(2,1)S(1)}) custom-call(s32[3]{0:T(128)S(1)} %add_add_fusion.ids, bf16[3,1024,512]{2,1,0:T(8,128)(2,1)} %get-tuple-element.70.low_ref, bf16[1024,512]{1,0:T(8,128)(2,1)S(1)} %copy-done.8, bf16[1024,2048]{1,0:T(8,128)(2,1)} %get-tuple-element.71.hid_ref, ...), custom_call_target="tpu_custom_call" | custom-call | flops 5000000000 | bytes 17000000 | tf_op jit(solution)/shard_map/weight_grads/pallas_call | solution.py:350
  314.4 1.8 fusion.40
  320.0 36.0 %attend_back.1 = f32[1024,512]{1,0:T(8,128)} custom-call(s32[3]{0:T(128)S(1)} %add_add_fusion.1.ids, bf16[4,1024,512]{2,1,0:T(8,128)(2,1)} %x_ref.11, bf16[8,4,64,384]{3,2,1,0:T(8,128)(2,1)} %bitcast.117, bf16[4,1024,128]{2,1,0:T(8,128)(2,1)S(1)} %copy-done.2, bf16[4,1024,128]{2,1,0:T(8,128)(2,1)S(1)} %copy-done, bf16[4,1024,128]{2,1,0:T(8,128)(2,1)S(1)} %copy-done.12, ...), custom_call_target="tpu_custom_call" | custom-call | flops 20000000000 | bytes 12000000 | tf_op jit(solution)/shard_map/attend_back/pallas_call | solution.py:464
  358.9 2.4 collective-permute-start.24
  362.0 8.7 %collective-permute-done.24 = bf16[8,64,384]{2,1,0:T(8,128)(2,1)S(1)} collective-permute-done((bf16[8,64,384]{2,1,0:T(8,128)(2,1)S(1)}, bf16[8,64,384]{2,1,0:T(8,128)(2,1)S(1)}, u32[]{:S(2)}, u32[]{:S(2)}) %collective-permute-start.24) | collective-permute-done | bytes 393248 | tf_op jit(solution)/shard_map/ppermute | solution.py:40
  370.8 1.8 collective-permute-start.25
  373.5 5.2 %collective-permute-done.25 = bf16[4,64,384]{2,1,0:T(8,128)(2,1)S(1)} collective-permute-done((bf16[4,64,384]{2,1,0:T(8,128)(2,1)S(1)}, bf16[4,64,384]{2,1,0:T(8,128)(2,1)S(1)}, u32[]{:S(2)}, u32[]{:S(2)}) %collective-permute-start.25) | collective-permute-done | bytes 196640 | tf_op jit(solution)/shard_map/ppermute | solution.py:40
  379.5 5.3 %collective-permute-done.26 = bf16[2,64,384]{2,1,0:T(8,128)(2,1)S(1)} collective-permute-done((bf16[2,64,384]{2,1,0:T(8,128)(2,1)S(1)}, bf16[2,64,384]{2,1,0:T(8,128)(2,1)S(1)}, u32[]{:S(2)}, u32[]{:S(2)}) %collective-permute-start.26) | collective-permute-done | bytes 98336 | tf_op jit(solution)/shard_map/ppermute | solution.py:40
  384.7 1.6 collective-permute-start.17
  386.4 2.1 collective-permute-done.34
  388.5 2.3 collective-permute-start.15
  391.6 1.7 collective-permute-start.35
  393.4 1.7 fusion
  396.5 15.9 %collective-permute-done.27 = bf16[1,64,384]{2,1,0:T(8,128)(2,1)S(1)} collective-permute-done((bf16[1,64,384]{2,1,0:T(8,128)(2,1)S(1)}, bf16[1,64,384]{2,1,0:T(8,128)(2,1)S(1)}, u32[]{:S(2)}, u32[]{:S(2)}) %collective-permute-start.27) | collective-permute-done | bytes 49184 | tf_op jit(solution)/shard_map/ppermute | solution.py:40
  414.3 1.6 reshape.478
  418.1 15.2 %collective-permute-start.36 = (bf16[2,64,512]{2,1,0:T(8,128)(2,1)S(1)}, bf16[2,64,512]{2,1,0:T(8,128)(2,1)S(1)}, u32[]{:S(2)}, u32[]{:S(2)}) collective-permute-start(bf16[2,64,512]{2,1,0:T(8,128)(2,1)S(1)} %slice.233), channel_id=1, source_target_pairs={{0,2},{1,3},{2,0},{3,1},{4,6},{5,7},{6,4},{7,5},{8,10},{9,11},{10,... | collective-permute-start | bytes 393224 | tf_op jit(solution)/shard_map/ppermute | solution.py:40
  433.3 1.9 multiply_subtract_fusion.2
  436.7 1.6 collective-permute-start.16
  438.3 2.8 collective-permute-start.37
  441.4 50.4 %collective-permute-done.37 = bf16[1,64,512]{2,1,0:T(8,128)(2,1)S(1)} collective-permute-done((bf16[1,64,512]{2,1,0:T(8,128)(2,1)S(1)}, bf16[1,64,512]{2,1,0:T(8,128)(2,1)S(1)}, u32[]{:S(2)}, u32[]{:S(2)}) %collective-permute-start.37) | collective-permute-done | bytes 65568 | tf_op jit(solution)/shard_map/ppermute | solution.py:40
  493.4 3.2 fusion.1
  497.1 1.7 collective-permute-done.30
  499.0 2.3 pad_maximum_fusion.1
  501.3 4.8 collective-permute-done.31
  506.3 3.9 pad_maximum_fusion
  (289 shorter events, 65.9 us)
Async XLA Ops:
  1.7 41.3 %collective-permute-start = (bf16[1,64,384]{2,1,0:T(8,128)(2,1)S(1)}, bf16[1,64,384]{2,1,0:T(8,128)(2,1)S(1)}, u32[]{:S(2)}, u32[]{:S(2)}) collective-permute-start(bf16[1,64,384]{2,1,0:T(8,128)(2,1)S(1)} %broadcast_in_dim_reshape.3), channel_id=1, source_target_pairs={{0,1},{1,0},{2,3},{3,2},{4,5},{5,4},{6,7},{7,6},{8,9},{9,8},{10,11... | collective-permute-start | bytes 147464 | tf_op jit(solution)/shard_map/ppermute | solution.py:40
  6.3 38.0 %collective-permute-start.10 = (bf16[1,64,512]{2,1,0:T(8,128)(2,1)S(1)}, bf16[1,64,512]{2,1,0:T(8,128)(2,1)S(1)}, u32[]{:S(2)}, u32[]{:S(2)}) collective-permute-start(bf16[1,64,512]{2,1,0:T(8,128)(2,1)S(1)} %get-tuple-element.155), channel_id=1, source_target_pairs={{0,1},{1,0},{2,3},{3,2},{4,5},{5,4},{6,7},{7,6},{8,9},{9,8},{10,11... | collective-permute-start | bytes 196616 | tf_op jit(solution)/shard_map/ppermute | solution.py:40
  8.7 38.7 %collective-permute-start.5 = (bf16[1,64,640]{2,1,0:T(8,128)(2,1)S(1)}, bf16[1,64,640]{2,1,0:T(8,128)(2,1)S(1)}, u32[]{:S(2)}, u32[]{:S(2)}) collective-permute-start(bf16[1,64,640]{2,1,0:T(8,128)(2,1)S(1)} %get-tuple-element.198), channel_id=1, source_target_pairs={{0,1},{1,0},{2,3},{3,2},{4,5},{5,4},{6,7},{7,6},{8,9},{9,8},{10,11... | collective-permute-start | bytes 245768 | tf_op jit(solution)/shard_map/ppermute | solution.py:40
  42.1 145.5 %copy-start.1 = (bf16[4,1024,128]{2,1,0:T(8,128)(2,1)}, bf16[4,1024,128]{2,1,0:T(8,128)(2,1)S(1)}, u32[]{:S(2)}) copy-start(bf16[4,1024,128]{2,1,0:T(8,128)(2,1)S(1)} %get-tuple-element.183.qf_ref) | copy-start | bytes 3145732
  43.0 13.4 %collective-permute-start.1 = (bf16[2,64,384]{2,1,0:T(8,128)(2,1)S(1)}, bf16[2,64,384]{2,1,0:T(8,128)(2,1)S(1)}, u32[]{:S(2)}, u32[]{:S(2)}) collective-permute-start(bf16[2,64,384]{2,1,0:T(8,128)(2,1)S(1)} %pad_maximum_fusion.10), channel_id=1, source_target_pairs={{0,2},{1,3},{2,0},{3,1},{4,6},{5,7},{6,4},{7,5},{8,10},{9,11},{10,... | collective-permute-start | bytes 294920 | tf_op jit(solution)/shard_map/ppermute | solution.py:40
  44.3 14.7 %collective-permute-start.11 = (bf16[2,64,512]{2,1,0:T(8,128)(2,1)S(1)}, bf16[2,64,512]{2,1,0:T(8,128)(2,1)S(1)}, u32[]{:S(2)}, u32[]{:S(2)}) collective-permute-start(bf16[2,64,512]{2,1,0:T(8,128)(2,1)S(1)} %pad_maximum_fusion.9), channel_id=1, source_target_pairs={{0,2},{1,3},{2,0},{3,1},{4,6},{5,7},{6,4},{7,5},{8,10},{9,11},{10,... | collective-permute-start | bytes 393224 | tf_op jit(solution)/shard_map/ppermute | solution.py:40
  47.4 13.3 %collective-permute-start.6 = (bf16[2,64,640]{2,1,0:T(8,128)(2,1)S(1)}, bf16[2,64,640]{2,1,0:T(8,128)(2,1)S(1)}, u32[]{:S(2)}, u32[]{:S(2)}) collective-permute-start(bf16[2,64,640]{2,1,0:T(8,128)(2,1)S(1)} %pad_maximum_fusion.8), channel_id=1, source_target_pairs={{0,2},{1,3},{2,0},{3,1},{4,6},{5,7},{6,4},{7,5},{8,10},{9,11},{10,... | collective-permute-start | bytes 491528 | tf_op jit(solution)/shard_map/ppermute | solution.py:40
  56.4 6.2 %collective-permute-start.2 = (bf16[4,64,384]{2,1,0:T(8,128)(2,1)S(1)}, bf16[4,64,384]{2,1,0:T(8,128)(2,1)S(1)}, u32[]{:S(2)}, u32[]{:S(2)}) collective-permute-start(bf16[4,64,384]{2,1,0:T(8,128)(2,1)S(1)} %pad_maximum_fusion.7), channel_id=1, source_target_pairs={{0,8},{4,12},{8,0},{12,4},{16,24},{20,28},{24,16},{28,20},{1,9},{5... | collective-permute-start | bytes 589832 | tf_op jit(solution)/shard_map/ppermute | solution.py:40
  59.0 8.9 %collective-permute-start.12 = (bf16[4,64,512]{2,1,0:T(8,128)(2,1)S(1)}, bf16[4,64,512]{2,1,0:T(8,128)(2,1)S(1)}, u32[]{:S(2)}, u32[]{:S(2)}) collective-permute-start(bf16[4,64,512]{2,1,0:T(8,128)(2,1)S(1)} %pad_maximum_fusion.6), channel_id=1, source_target_pairs={{0,16},{4,20},{8,24},{12,28},{16,0},{20,4},{24,8},{28,12},{1,17},{... | collective-permute-start | bytes 786440 | tf_op jit(solution)/shard_map/ppermute | solution.py:40
  60.8 10.7 %collective-permute-start.7 = (bf16[4,64,640]{2,1,0:T(8,128)(2,1)S(1)}, bf16[4,64,640]{2,1,0:T(8,128)(2,1)S(1)}, u32[]{:S(2)}, u32[]{:S(2)}) collective-permute-start(bf16[4,64,640]{2,1,0:T(8,128)(2,1)S(1)} %pad_maximum_fusion.5), channel_id=1, source_target_pairs={{0,8},{4,12},{8,0},{12,4},{16,24},{20,28},{24,16},{28,20},{1,9},{5... | collective-permute-start | bytes 983048 | tf_op jit(solution)/shard_map/ppermute | solution.py:40
  62.6 13.8 %collective-permute-start.3 = (bf16[8,64,384]{2,1,0:T(8,128)(2,1)S(1)}, bf16[8,64,384]{2,1,0:T(8,128)(2,1)S(1)}, u32[]{:S(2)}, u32[]{:S(2)}) collective-permute-start(bf16[8,64,384]{2,1,0:T(8,128)(2,1)S(1)} %pad_maximum_fusion.4), channel_id=1, source_target_pairs={{0,16},{4,20},{8,24},{12,28},{16,0},{20,4},{24,8},{28,12},{1,17},{... | collective-permute-start | bytes 1179656 | tf_op jit(solution)/shard_map/ppermute | solution.py:40
  68.0 12.4 %collective-permute-start.13 = (bf16[8,64,512]{2,1,0:T(8,128)(2,1)S(1)}, bf16[8,64,512]{2,1,0:T(8,128)(2,1)S(1)}, u32[]{:S(2)}, u32[]{:S(2)}) collective-permute-start(bf16[8,64,512]{2,1,0:T(8,128)(2,1)S(1)} %pad_maximum_fusion.3), channel_id=1, source_target_pairs={{0,8},{4,12},{8,0},{12,4},{16,24},{20,28},{24,16},{28,20},{1,9},{5... | collective-permute-start | bytes 1572872 | tf_op jit(solution)/shard_map/ppermute | solution.py:40
  71.6 16.4 %collective-permute-start.8 = (bf16[8,64,640]{2,1,0:T(8,128)(2,1)S(1)}, bf16[8,64,640]{2,1,0:T(8,128)(2,1)S(1)}, u32[]{:S(2)}, u32[]{:S(2)}) collective-permute-start(bf16[8,64,640]{2,1,0:T(8,128)(2,1)S(1)} %pad_maximum_fusion.2), channel_id=1, source_target_pairs={{0,16},{4,20},{8,24},{12,28},{16,0},{20,4},{24,8},{28,12},{1,17},{... | collective-permute-start | bytes 1966088 | tf_op jit(solution)/shard_map/ppermute | solution.py:40
  76.6 12.4 %collective-permute-start.4 = (bf16[16,64,384]{2,1,0:T(8,128)(2,1)S(1)}, bf16[16,64,384]{2,1,0:T(8,128)(2,1)S(1)}, u32[]{:S(2)}, u32[]{:S(2)}) collective-permute-start(bf16[16,64,384]{2,1,0:T(8,128)(2,1)S(1)} %get-tuple-element.178), channel_id=1, source_target_pairs={{0,4},{4,0},{8,12},{12,8},{16,20},{20,16},{24,28},{28,24},{1,5},{5... | collective-permute-start | bytes 2359304 | tf_op jit(solution)/shard_map/ppermute | solution.py:40
  81.3 72.0 %collective-permute-start.14 = (bf16[16,64,512]{2,1,0:T(8,128)(2,1)S(1)}, bf16[16,64,512]{2,1,0:T(8,128)(2,1)S(1)}, u32[]{:S(2)}, u32[]{:S(2)}) collective-permute-start(bf16[16,64,512]{2,1,0:T(8,128)(2,1)S(1)} %get-tuple-element.176), channel_id=1, source_target_pairs={{0,4},{4,0},{8,12},{12,8},{16,20},{20,16},{24,28},{28,24},{1,5},{5... | collective-permute-start | bytes 3145736 | tf_op jit(solution)/shard_map/ppermute | solution.py:40
  89.0 65.5 %collective-permute-start.9 = (bf16[16,64,640]{2,1,0:T(8,128)(2,1)S(1)}, bf16[16,64,640]{2,1,0:T(8,128)(2,1)S(1)}, u32[]{:S(2)}, u32[]{:S(2)}) collective-permute-start(bf16[16,64,640]{2,1,0:T(8,128)(2,1)S(1)} %get-tuple-element.174), channel_id=1, source_target_pairs={{0,4},{4,0},{8,12},{12,8},{16,20},{20,16},{24,28},{28,24},{1,5},{5... | collective-permute-start | bytes 3932168 | tf_op jit(solution)/shard_map/ppermute | solution.py:40
  229.5 49.0 %copy-start.18 = (bf16[1024,512]{1,0:T(8,128)(2,1)S(1)}, bf16[1024,512]{1,0:T(8,128)(2,1)}, u32[]{:S(2)}) copy-start(bf16[1024,512]{1,0:T(8,128)(2,1)} %copy-done.17) | copy-start | bytes 3145732
  269.4 122.2 %collective-permute-start.21 = (bf16[1024,512]{1,0:T(8,128)(2,1)}, bf16[1024,512]{1,0:T(8,128)(2,1)}, u32[]{:S(2)}, u32[]{:S(2)}) collective-permute-start(bf16[1024,512]{1,0:T(8,128)(2,1)} %convert_element_type.210), channel_id=1, source_target_pairs={{1,2},{2,1},{5,6},{6,5},{9,10},{10,9},{13,14},{14,13},{17,18},{18,... | collective-permute-start | bytes 3145736 | tf_op jit(solution)/shard_map/ppermute | solution.py:591
  271.1 124.1 %collective-permute-start.19 = (bf16[1024,512]{1,0:T(8,128)(2,1)}, bf16[1024,512]{1,0:T(8,128)(2,1)}, u32[]{:S(2)}, u32[]{:S(2)}) collective-permute-start(bf16[1024,512]{1,0:T(8,128)(2,1)} %convert_element_type.210), channel_id=1, source_target_pairs={{3,1},{0,2},{7,5},{4,6},{11,9},{8,10},{15,13},{12,14},{19,17},{16,... | collective-permute-start | bytes 3145736 | tf_op jit(solution)/shard_map/ppermute | solution.py:592
  316.5 41.0 %collective-permute-start.23 = (bf16[16,64,384]{2,1,0:T(8,128)(2,1)}, bf16[16,64,384]{2,1,0:T(8,128)(2,1)}, u32[]{:S(2)}, u32[]{:S(2)}) collective-permute-start(bf16[16,64,384]{2,1,0:T(8,128)(2,1)} %bitcast.101), channel_id=1, source_target_pairs={{0,4},{4,0},{8,12},{12,8},{16,20},{20,16},{24,28},{28,24},{1,5},{5... | collective-permute-start | bytes 2359304 | tf_op jit(solution)/shard_map/ppermute | solution.py:40
  316.5 75.1 %collective-permute-start.28 = (bf16[16,64,640]{2,1,0:T(8,128)(2,1)}, bf16[16,64,640]{2,1,0:T(8,128)(2,1)}, u32[]{:S(2)}, u32[]{:S(2)}) collective-permute-start(bf16[16,64,640]{2,1,0:T(8,128)(2,1)} %bitcast.100), channel_id=1, source_target_pairs={{0,4},{4,0},{8,12},{12,8},{16,20},{20,16},{24,28},{28,24},{1,5},{5... | collective-permute-start | bytes 3932168 | tf_op jit(solution)/shard_map/ppermute | solution.py:40
  318.6 54.0 %collective-permute-start.33 = (bf16[16,64,512]{2,1,0:T(8,128)(2,1)}, bf16[16,64,512]{2,1,0:T(8,128)(2,1)S(1)}, u32[]{:S(2)}, u32[]{:S(2)}) collective-permute-start(bf16[16,64,512]{2,1,0:T(8,128)(2,1)} %bitcast.34), channel_id=1, source_target_pairs={{0,4},{4,0},{8,12},{12,8},{16,20},{20,16},{24,28},{28,24},{1,5},{5... | collective-permute-start | bytes 3145736 | tf_op jit(solution)/shard_map/ppermute | solution.py:40
  320.0 36.8 %copy-start.45 = (f32[2,2,8]{2,1,0:T(2,128)S(1)}, f32[2,2,8]{2,1,0:T(2,128)}, u32[]{:S(2)}) copy-start(f32[2,2,8]{2,1,0:T(2,128)} %param.36) | copy-start | bytes 388
  320.0 36.8 %copy-start.55 = (f32[2,2,8]{2,1,0:T(2,128)S(1)}, f32[2,2,8]{2,1,0:T(2,128)}, u32[]{:S(2)}) copy-start(f32[2,2,8]{2,1,0:T(2,128)} %param.44) | copy-start | bytes 388
  320.0 37.4 %copy-start.30 = (bf16[4,4,64,384]{3,2,1,0:T(8,128)(2,1)S(1)}, bf16[4,4,64,384]{3,2,1,0:T(8,128)(2,1)}, u32[]{:S(2)}) copy-start(bf16[4,4,64,384]{3,2,1,0:T(8,128)(2,1)} %get-tuple-element.172) | copy-start | bytes 2359300
  358.9 11.7 %collective-permute-start.24 = (bf16[8,64,384]{2,1,0:T(8,128)(2,1)S(1)}, bf16[8,64,384]{2,1,0:T(8,128)(2,1)S(1)}, u32[]{:S(2)}, u32[]{:S(2)}) collective-permute-start(bf16[8,64,384]{2,1,0:T(8,128)(2,1)S(1)} %slice.211), channel_id=1, source_target_pairs={{0,16},{4,20},{8,24},{12,28},{16,0},{20,4},{24,8},{28,12},{1,17},{... | collective-permute-start | bytes 1179656 | tf_op jit(solution)/shard_map/ppermute | solution.py:40
  370.8 7.9 %collective-permute-start.25 = (bf16[4,64,384]{2,1,0:T(8,128)(2,1)S(1)}, bf16[4,64,384]{2,1,0:T(8,128)(2,1)S(1)}, u32[]{:S(2)}, u32[]{:S(2)}) collective-permute-start(bf16[4,64,384]{2,1,0:T(8,128)(2,1)S(1)} %slice.213), channel_id=1, source_target_pairs={{0,8},{4,12},{8,0},{12,4},{16,24},{20,28},{24,16},{28,20},{1,9},{5... | collective-permute-start | bytes 589832 | tf_op jit(solution)/shard_map/ppermute | solution.py:40
  373.1 15.4 %collective-permute-start.34 = (bf16[8,64,512]{2,1,0:T(8,128)(2,1)S(1)}, bf16[8,64,512]{2,1,0:T(8,128)(2,1)S(1)}, u32[]{:S(2)}, u32[]{:S(2)}) collective-permute-start(bf16[8,64,512]{2,1,0:T(8,128)(2,1)S(1)} %slice.229), channel_id=1, source_target_pairs={{0,8},{4,12},{8,0},{12,4},{16,24},{20,28},{24,16},{28,20},{1,9},{5... | collective-permute-start | bytes 1572872 | tf_op jit(solution)/shard_map/ppermute | solution.py:40
  378.8 6.0 %collective-permute-start.26 = (bf16[2,64,384]{2,1,0:T(8,128)(2,1)S(1)}, bf16[2,64,384]{2,1,0:T(8,128)(2,1)S(1)}, u32[]{:S(2)}, u32[]{:S(2)}) collective-permute-start(bf16[2,64,384]{2,1,0:T(8,128)(2,1)S(1)} %slice.215), channel_id=1, source_target_pairs={{0,2},{1,3},{2,0},{3,1},{4,6},{5,7},{6,4},{7,5},{8,10},{9,11},{10,... | collective-permute-start | bytes 294920 | tf_op jit(solution)/shard_map/ppermute | solution.py:40
  384.7 33.3 %collective-permute-start.17 = (bf16[1024,512]{1,0:T(8,128)(2,1)S(1)}, bf16[1024,512]{1,0:T(8,128)(2,1)}, u32[]{:S(2)}, u32[]{:S(2)}) collective-permute-start(bf16[1024,512]{1,0:T(8,128)(2,1)S(1)} %copy-done.4), channel_id=1, source_target_pairs={{1,2},{2,1},{5,6},{6,5},{9,10},{10,9},{13,14},{14,13},{17,18},{18,... | collective-permute-start | bytes 3145736 | tf_op jit(solution)/shard_map/ppermute | solution.py:591
  388.5 46.8 %collective-permute-start.15 = (bf16[1024,512]{1,0:T(8,128)(2,1)S(1)}, bf16[1024,512]{1,0:T(8,128)(2,1)}, u32[]{:S(2)}, u32[]{:S(2)}) collective-permute-start(bf16[1024,512]{1,0:T(8,128)(2,1)S(1)} %copy-done.4), channel_id=1, source_target_pairs={{3,1},{0,2},{7,5},{4,6},{11,9},{8,10},{15,13},{12,14},{19,17},{16,... | collective-permute-start | bytes 3145736 | tf_op jit(solution)/shard_map/ppermute | solution.py:592
  391.6 20.7 %collective-permute-start.27 = (bf16[1,64,384]{2,1,0:T(8,128)(2,1)S(1)}, bf16[1,64,384]{2,1,0:T(8,128)(2,1)S(1)}, u32[]{:S(2)}, u32[]{:S(2)}) collective-permute-start(bf16[1,64,384]{2,1,0:T(8,128)(2,1)S(1)} %slice.217), channel_id=1, source_target_pairs={{0,1},{1,0},{2,3},{3,2},{4,5},{5,4},{6,7},{7,6},{8,9},{9,8},{10,11... | collective-permute-start | bytes 147464 | tf_op jit(solution)/shard_map/ppermute | solution.py:40
  391.6 24.2 %collective-permute-start.35 = (bf16[4,64,512]{2,1,0:T(8,128)(2,1)}, bf16[4,64,512]{2,1,0:T(8,128)(2,1)}, u32[]{:S(2)}, u32[]{:S(2)}) collective-permute-start(bf16[4,64,512]{2,1,0:T(8,128)(2,1)} %slice.231), channel_id=1, source_target_pairs={{0,16},{4,20},{8,24},{12,28},{16,0},{20,4},{24,8},{28,12},{1,17},{... | collective-permute-start | bytes 786440 | tf_op jit(solution)/shard_map/ppermute | solution.py:40
  395.2 98.2 %collective-permute-start.22 = (bf16[1024,512]{1,0:T(8,128)(2,1)}, bf16[1024,512]{1,0:T(8,128)(2,1)}, u32[]{:S(2)}, u32[]{:S(2)}) collective-permute-start(bf16[1024,512]{1,0:T(8,128)(2,1)} %collective-permute-done.21), channel_id=1, source_target_pairs={{1,0},{2,3},{5,4},{6,7},{9,8},{10,11},{13,12},{14,15},{17,16},{18,... | collective-permute-start | bytes 3145736 | tf_op jit(solution)/shard_map/ppermute | solution.py:593
  412.4 81.0 %collective-permute-start.20 = (bf16[1024,512]{1,0:T(8,128)(2,1)}, bf16[1024,512]{1,0:T(8,128)(2,1)}, u32[]{:S(2)}, u32[]{:S(2)}) collective-permute-start(bf16[1024,512]{1,0:T(8,128)(2,1)} %collective-permute-done.19), channel_id=1, source_target_pairs={{1,0},{2,3},{5,4},{6,7},{9,8},{10,11},{13,12},{14,15},{17,16},{18,... | collective-permute-start | bytes 3145736 | tf_op jit(solution)/shard_map/ppermute | solution.py:594
  415.9 22.4 %collective-permute-start.29 = (bf16[8,64,640]{2,1,0:T(8,128)(2,1)S(1)}, bf16[8,64,640]{2,1,0:T(8,128)(2,1)S(1)}, u32[]{:S(2)}, u32[]{:S(2)}) collective-permute-start(bf16[8,64,640]{2,1,0:T(8,128)(2,1)S(1)} %slice.219), channel_id=1, source_target_pairs={{0,16},{4,20},{8,24},{12,28},{16,0},{20,4},{24,8},{28,12},{1,17},{... | collective-permute-start | bytes 1966088 | tf_op jit(solution)/shard_map/ppermute | solution.py:40
  418.0 74.6 %copy-start.33 = (f32[512,64]{0,1:T(8,128)S(1)}, f32[512,64]{0,1:T(8,128)}, u32[]{:S(2)}) copy-start(f32[512,64]{0,1:T(8,128)} %param.35) | copy-start | bytes 393220
  418.0 74.6 %copy-start.35 = (f32[512,64]{0,1:T(8,128)S(1)}, f32[512,64]{0,1:T(8,128)}, u32[]{:S(2)}) copy-start(f32[512,64]{0,1:T(8,128)} %param.43) | copy-start | bytes 393220
  418.0 74.6 %copy-start.36 = (f32[512,64]{0,1:T(8,128)S(1)}, f32[512,64]{0,1:T(8,128)}, u32[]{:S(2)}) copy-start(f32[512,64]{0,1:T(8,128)} %param.51) | copy-start | bytes 393220
  418.1 18.6 %collective-permute-start.36 = (bf16[2,64,512]{2,1,0:T(8,128)(2,1)S(1)}, bf16[2,64,512]{2,1,0:T(8,128)(2,1)S(1)}, u32[]{:S(2)}, u32[]{:S(2)}) collective-permute-start(bf16[2,64,512]{2,1,0:T(8,128)(2,1)S(1)} %slice.233), channel_id=1, source_target_pairs={{0,2},{1,3},{2,0},{3,1},{4,6},{5,7},{6,4},{7,5},{8,10},{9,11},{10,... | collective-permute-start | bytes 393224 | tf_op jit(solution)/shard_map/ppermute | solution.py:40
  433.3 60.1 %copy-start.31 = (f32[1024,512]{1,0:T(8,128)S(1)}, f32[1024,512]{1,0:T(8,128)}, u32[]{:S(2)}) copy-start(f32[1024,512]{1,0:T(8,128)} %attend_back.1) | copy-start | bytes 6291460
  435.2 58.2 %copy-start.27 = (f32[1024,512]{1,0:T(8,128)S(1)}, f32[1024,512]{1,0:T(8,128)}, u32[]{:S(2)}) copy-start(f32[1024,512]{1,0:T(8,128)} %get-tuple-element.62) | copy-start | bytes 6291460
  435.2 61.4 %collective-permute-start.18 = (bf16[1024,512]{1,0:T(8,128)(2,1)}, bf16[1024,512]{1,0:T(8,128)(2,1)S(1)}, u32[]{:S(2)}, u32[]{:S(2)}) collective-permute-start(bf16[1024,512]{1,0:T(8,128)(2,1)} %collective-permute-done.17), channel_id=1, source_target_pairs={{1,0},{2,3},{5,4},{6,7},{9,8},{10,11},{13,12},{14,15},{17,16},{18,... | collective-permute-start | bytes 3145736 | tf_op jit(solution)/shard_map/ppermute | solution.py:593
  436.7 60.0 %collective-permute-start.16 = (bf16[1024,512]{1,0:T(8,128)(2,1)}, bf16[1024,512]{1,0:T(8,128)(2,1)S(1)}, u32[]{:S(2)}, u32[]{:S(2)}) collective-permute-start(bf16[1024,512]{1,0:T(8,128)(2,1)} %collective-permute-done.15), channel_id=1, source_target_pairs={{1,0},{2,3},{5,4},{6,7},{9,8},{10,11},{13,12},{14,15},{17,16},{18,... | collective-permute-start | bytes 3145736 | tf_op jit(solution)/shard_map/ppermute | solution.py:594
  438.3 53.4 %collective-permute-start.37 = (bf16[1,64,512]{2,1,0:T(8,128)(2,1)S(1)}, bf16[1,64,512]{2,1,0:T(8,128)(2,1)S(1)}, u32[]{:S(2)}, u32[]{:S(2)}) collective-permute-start(bf16[1,64,512]{2,1,0:T(8,128)(2,1)S(1)} %slice.235), channel_id=1, source_target_pairs={{0,1},{1,0},{2,3},{3,2},{4,5},{5,4},{6,7},{7,6},{8,9},{9,8},{10,11... | collective-permute-start | bytes 196616 | tf_op jit(solution)/shard_map/ppermute | solution.py:40
  491.7 7.1 %collective-permute-start.30 = (bf16[4,64,640]{2,1,0:T(8,128)(2,1)S(1)}, bf16[4,64,640]{2,1,0:T(8,128)(2,1)S(1)}, u32[]{:S(2)}, u32[]{:S(2)}) collective-permute-start(bf16[4,64,640]{2,1,0:T(8,128)(2,1)S(1)} %slice.221), channel_id=1, source_target_pairs={{0,8},{4,12},{8,0},{12,4},{16,24},{20,28},{24,16},{28,20},{1,9},{5... | collective-permute-start | bytes 983048 | tf_op jit(solution)/shard_map/ppermute | solution.py:40
  498.9 7.1 %collective-permute-start.31 = (bf16[2,64,640]{2,1,0:T(8,128)(2,1)S(1)}, bf16[2,64,640]{2,1,0:T(8,128)(2,1)S(1)}, u32[]{:S(2)}, u32[]{:S(2)}) collective-permute-start(bf16[2,64,640]{2,1,0:T(8,128)(2,1)S(1)} %slice.223), channel_id=1, source_target_pairs={{0,2},{1,3},{2,0},{3,1},{4,6},{5,7},{6,4},{7,5},{8,10},{9,11},{10,... | collective-permute-start | bytes 491528 | tf_op jit(solution)/shard_map/ppermute | solution.py:40
  506.1 4.5 collective-permute-start.32
  (55 other events, 550.3 us)
